TPU v7x, 32 devices: a whole 2x2x4 slice. The times are simulated.
32 devices in a mesh: groups: 2 (over y), expert: 4 (over z), dp: 2 (over x), tensor: 2 (over core).
Axes of the slice: x: 2, y: 2, z: 4, core: 2. Of those that a mesh axis runs over, the one named last changes fastest.
Arguments:
- x_res: bfloat16 [2, 256, 1440], P(None, ('groups', 'expert', 'dp')), parts along dimension 1, may hold values from -6 to 6
- query_new: bfloat16 [2, 256, 2048], P(None, ('groups', 'expert', 'dp'), 'tensor'), parts along dimension 1, may hold values from -8 to 8
- key_new: bfloat16 [2, 256, 256], P(None, ('groups', 'expert', 'dp'), 'tensor'), parts along dimension 1, may hold values from -6 to 6
- value_new: bfloat16 [2, 256, 256], P(None, ('groups', 'expert', 'dp'), 'tensor'), parts along dimension 1, may hold values from -6 to 6
- key_cache: bfloat16 [256, 64, 256], P(('groups', 'expert', 'dp'), None, 'tensor'), parts along dimension 0, may hold values from -8 to 8
- value_cache: bfloat16 [256, 64, 256], P(('groups', 'expert', 'dp'), None, 'tensor'), parts along dimension 0, may hold values from -6 to 6
- lengths: int32 [256], P(('groups', 'expert', 'dp')), parts along dimension 0, may hold values from 2 to 64, as said below
- routes: int32 [2, 256, 4], P(None, ('groups', 'expert', 'dp')), parts along dimension 1, may hold values from 0 to 7, all different within a row; in each aligned block of 16 rows (0 to 15, 16 to 31, ..., all dimensions but the last counted through in order) at most 16 rows name the same one
- route_weight: float32 [2, 256, 4], P(None, ('groups', 'expert', 'dp')), parts along dimension 1, may hold values from 0.2 to 1
- norm_gain: float32 [1440], replicated, may hold values from 0.1 to 1.9
- out_weight: bfloat16 [2048, 1440], P('tensor', 'dp'), may hold values from -0.125 to 0.125
- w_gate: bfloat16 [8, 1440, 1440], P(None, 'expert', ('dp', 'tensor')), may hold values from -0.15625 to 0.15625
- w_up: bfloat16 [8, 1440, 1440], P(None, 'expert', ('dp', 'tensor')), may hold values from -0.15625 to 0.15625
- w_down: bfloat16 [8, 1440, 1440], P(None, 'expert', ('dp', 'tensor')), may hold values from -0.15625 to 0.15625
Outputs:
- layer_out: bfloat16 [2, 256, 1440], P(None, ('groups', 'expert', 'dp'), 'tensor'), parts along dimension 1
There are 2 independent parts, one for each index of `groups`. A program takes and returns all parts, laid end to end along the dimension named above; an argument that names none is the same for every part. Nothing has to cross between parts.
Inputs may be any that keep to these rules, and one draw needn't show every extreme that they name: `routes`: each token names 4 different experts. Within one step the 16 tokens of one device (an aligned block of rows) name any one expert at most 16 times, a bound that some block reaches. `lengths`: some sequence uses all 64 positions.
All inputs are finite; a program needn't handle non-finite values.
Results may differ from a plain program's by a relative error of at most 0.0054.
Values may be sent and summed in bfloat16 or wider, within the bound.
A program may use at most 128 MiB of HBM per device.

v0:
```python
import jax
import jax.numpy as jnp
from jax import lax
from jax.sharding import PartitionSpec as P

HEAD_DIM = 64


def attend(query_row, key_cache, value_cache, key_new, value_new, lengths, moment):
    batch_size = query_row.shape[0]
    groups = key_cache.shape[2] // HEAD_DIM
    per_group = query_row.shape[1] // (groups * HEAD_DIM)
    window = key_cache.shape[1]
    new_count = key_new.shape[0]
    queries = query_row.reshape(batch_size, groups, per_group, HEAD_DIM)
    old_keys = key_cache.reshape(batch_size, window, groups, HEAD_DIM)
    old_values = value_cache.reshape(batch_size, window, groups, HEAD_DIM)
    new_keys = key_new.reshape(new_count, batch_size, groups, HEAD_DIM)
    new_values = value_new.reshape(new_count, batch_size, groups, HEAD_DIM)
    factor = HEAD_DIM ** (-0.5)
    old_scores = (
        jnp.einsum("bgrd,bcgd->bgrc", queries, old_keys, preferred_element_type=jnp.float32)
        * factor
    )
    new_scores = (
        jnp.einsum("bgrd,sbgd->bgrs", queries, new_keys, preferred_element_type=jnp.float32)
        * factor
    )
    old_valid = (jnp.arange(window)[None, :] < lengths[:, None])[:, None, None, :]
    new_valid = (jnp.arange(new_count) <= moment)[None, None, None, :]
    scores = jnp.concatenate(
        [jnp.where(old_valid, old_scores, -jnp.inf), jnp.where(new_valid, new_scores, -jnp.inf)],
        axis=-1,
    )
    highest = jnp.max(scores, axis=-1, keepdims=True)
    powers = jnp.exp(scores - highest)
    weights = (powers / jnp.sum(powers, axis=-1, keepdims=True)).astype(jnp.bfloat16)
    attended = jnp.einsum(
        "bgrc,bcgd->bgrd", weights[..., :window], old_values, preferred_element_type=jnp.float32
    )
    attended = attended + jnp.einsum(
        "bgrs,sbgd->bgrd", weights[..., window:], new_values, preferred_element_type=jnp.float32
    )
    return attended.reshape(batch_size, groups * per_group * HEAD_DIM).astype(jnp.bfloat16)


def local(
    x_res,
    query_new,
    key_new,
    value_new,
    key_cache,
    value_cache,
    lengths,
    routes,
    route_weight,
    norm_gain,
    out_weight,
    w_gate,
    w_up,
    w_down,
):
    expert_count = lax.axis_size("expert")
    row_count = lax.axis_size("dp")
    half_count = lax.axis_size("tensor")
    total_experts = w_gate.shape[0]
    owned_count = total_experts // expert_count
    copies = row_count // owned_count
    tokens = x_res.shape[1]
    choose_k = routes.shape[2]
    capacity = 2 * max(1, tokens * choose_k // total_experts)
    slot_count = capacity // copies
    width = x_res.shape[2]
    row_part = w_gate.shape[1]
    col_part = w_gate.shape[2]
    sectioned = tuple(
        (
            matrix.reshape(expert_count, owned_count, row_part, col_part)
            for matrix in (w_gate, w_up, w_down)
        )
    )
    doubled = tuple((jnp.repeat(matrix, copies, axis=1) for matrix in sectioned))
    placed = (
        lax.all_to_all(
            lax.all_to_all(doubled[0], "expert", split_axis=0, concat_axis=2, tiled=True),
            "dp",
            split_axis=1,
            concat_axis=3,
            tiled=True,
        ),
        lax.all_to_all(
            lax.all_to_all(doubled[1], "expert", split_axis=0, concat_axis=2, tiled=True),
            "dp",
            split_axis=1,
            concat_axis=3,
            tiled=True,
        ),
        lax.all_to_all(
            lax.all_to_all(doubled[2], "expert", split_axis=0, concat_axis=2, tiled=True),
            "dp",
            split_axis=1,
            concat_axis=3,
            tiled=True,
        ),
    )
    gate_w, up_w, down_w = (matrix.reshape(width, -1) for matrix in placed)
    out_proj = lax.all_gather(out_weight, "dp", axis=1, tiled=True)
    lane_ids = jnp.arange(expert_count * row_count * slot_count, dtype=jnp.int32)
    half_width = width // half_count
    results = []
    for moment in range(query_new.shape[0]):
        attended = attend(
            query_new[moment], key_cache, value_cache, key_new, value_new, lengths, moment
        )
        partial_value = jnp.dot(attended, out_proj, preferred_element_type=jnp.float32)
        hidden_state = x_res[moment].astype(jnp.float32) + lax.psum(partial_value, "tensor")
        mean_square = jnp.mean(hidden_state * hidden_state, axis=-1, keepdims=True)
        normed = (hidden_state * lax.rsqrt(mean_square + 1e-05) * norm_gain).astype(jnp.bfloat16)
        chosen = routes[moment].reshape(-1)
        matches = (chosen[:, None] == jnp.arange(total_experts, dtype=jnp.int32)[None, :]).astype(
            jnp.int32
        )
        before = jnp.cumsum(matches, axis=0) - matches
        order_rank = jnp.sum(before * matches, axis=1)
        target = (
            chosen // owned_count * row_count
            + chosen % owned_count * copies
            + order_rank // slot_count
        )
        lane_of = target * slot_count + order_rank % slot_count
        selector = lane_of[:, None] == lane_ids[None, :]
        per_token = jnp.any(selector.reshape(tokens, choose_k, -1), axis=1)
        outgoing = jnp.dot(
            per_token.T.astype(jnp.bfloat16), normed, preferred_element_type=jnp.float32
        ).astype(jnp.bfloat16)
        arrived = lax.all_to_all(
            outgoing.reshape(expert_count * row_count, slot_count, width),
            ("expert", "dp"),
            split_axis=0,
            concat_axis=0,
            tiled=True,
        )
        slot_rows = arrived.reshape(-1, width)
        gate_act = jnp.dot(slot_rows, gate_w, preferred_element_type=jnp.float32)
        up_act = jnp.dot(slot_rows, up_w, preferred_element_type=jnp.float32)
        activated = (jax.nn.silu(gate_act) * up_act).astype(jnp.bfloat16)
        partial_out = lax.dot_general(
            activated, down_w, (((1,), (1,)), ((), ())), preferred_element_type=jnp.float32
        )
        expert_out = lax.psum(partial_out, "tensor").astype(jnp.bfloat16)
        out_width = expert_out.shape[1]
        returned = lax.all_to_all(
            expert_out.reshape(expert_count * row_count, slot_count, out_width),
            ("expert", "dp"),
            split_axis=0,
            concat_axis=0,
            tiled=True,
        )
        gathered = jnp.dot(
            selector.astype(jnp.bfloat16),
            returned.reshape(-1, out_width),
            preferred_element_type=jnp.float32,
        )
        gathered = gathered.reshape(tokens, choose_k, out_width)
        combined = jnp.sum(route_weight[moment][:, :, None] * gathered, axis=1)
        whole_out = (hidden_state + combined).astype(jnp.bfloat16)
        results.append(
            lax.dynamic_slice_in_dim(
                whole_out, lax.axis_index("tensor") * half_width, half_width, 1
            )
        )
    return jnp.stack(results)


def solution(mesh):
    in_specs = (
        P(None, ("groups", "expert", "dp"), None),
        P(None, ("groups", "expert", "dp"), "tensor"),
        P(None, ("groups", "expert", "dp"), "tensor"),
        P(None, ("groups", "expert", "dp"), "tensor"),
        P(("groups", "expert", "dp"), None, "tensor"),
        P(("groups", "expert", "dp"), None, "tensor"),
        P(("groups", "expert", "dp")),
        P(None, ("groups", "expert", "dp"), None),
        P(None, ("groups", "expert", "dp"), None),
        P(),
        P("tensor", "dp"),
        P(None, "expert", ("dp", "tensor")),
        P(None, "expert", ("dp", "tensor")),
        P(None, "expert", ("dp", "tensor")),
    )
    out_specs = P(None, ("groups", "expert", "dp"), "tensor")
    return jax.shard_map(local, mesh=mesh, in_specs=in_specs, out_specs=out_specs, check_vma=False)
```

profile of v0, /device:TPU:0, one launch (start us, length us, event | category | flops | bytes accessed | tf_op | source)
XLA Modules:
  0.0 347.4 jit_solution(16603315736505989659)
XLA Ops:
  6.5 57.2 %all_to_all.119 = bf16[4,2,360,360]{3,2,1,0:T(8,128)(2,1)} all-to-all(bf16[4,2,360,360]{3,2,1,0:T(8,128)(2,1)} %bitcast.136), channel_id=1, replica_groups=mesh['groups'=2,'expert'=4,'dp'=2,'tensor'=2] {'expert'}, dimensions={0} | all-to-all | bytes 4147200 | tf_op jit(solution)/shard_map/all_to_all | solution.py:99
  63.7 53.0 %all_to_all.120 = bf16[4,2,360,360]{3,2,1,0:T(8,128)(2,1)} all-to-all(bf16[4,2,360,360]{3,2,1,0:T(8,128)(2,1)S(1)} %bitcast.137), channel_id=1, replica_groups=mesh['groups'=2,'expert'=4,'dp'=2,'tensor'=2] {'expert'}, dimensions={0} | all-to-all | bytes 4147200 | tf_op jit(solution)/shard_map/all_to_all | solution.py:92
  116.8 3.8 %all-to-all-start.1 = ((bf16[4,2,360,360]{3,2,1,0:T(8,128)(2,1)}), bf16[4,2,360,360]{3,2,1,0:T(8,128)(2,1)S(1)}, u32[]{:S(2)}, u32[]{:S(2)}) async-start(bf16[4,2,360,360]{3,2,1,0:T(8,128)(2,1)} %bitcast.138), calls=%async_computation.1 | async-start | bytes 4423680 | tf_op jit(solution)/shard_map/all_to_all | solution.py:85
  126.2 1.7 fusion.85
  130.0 1.5 fusion.87
  132.8 3.3 copy.165
  136.2 34.2 %all-to-all-done.1 = bf16[4,2,360,360]{3,2,1,0:T(8,128)(2,1)S(1)} async-done(((bf16[4,2,360,360]{3,2,1,0:T(8,128)(2,1)}), bf16[4,2,360,360]{3,2,1,0:T(8,128)(2,1)S(1)}, u32[]{:S(2)}, u32[]{:S(2)}) %all-to-all-start.1) | async-done | bytes 2073632 | tf_op jit(solution)/shard_map/all_to_all | solution.py:85
  170.4 1.4 copy-done.3
  171.8 3.8 %all-to-all-start.6 = ((bf16[1,2,1440,360]{3,2,0,1:T(8,128)(2,1)}), bf16[1,2,1440,360]{3,2,0,1:T(8,128)(2,1)S(1)}, u32[]{:S(2)}, u32[]{:S(2)}) async-start(bf16[1,2,1440,360]{3,2,0,1:T(8,128)(2,1)} %bitcast.135), calls=%async_computation.6 | async-start | bytes 4423680 | tf_op jit(solution)/shard_map/all_to_all | solution.py:98
  177.0 3.3 copy.162
  180.3 20.8 %all-to-all-done.6 = bf16[1,2,1440,360]{3,2,0,1:T(8,128)(2,1)S(1)} async-done(((bf16[1,2,1440,360]{3,2,0,1:T(8,128)(2,1)}), bf16[1,2,1440,360]{3,2,0,1:T(8,128)(2,1)S(1)}, u32[]{:S(2)}, u32[]{:S(2)}) %all-to-all-start.6) | async-done | bytes 2073632 | tf_op jit(solution)/shard_map/all_to_all | solution.py:98
  202.5 4.9 %all-to-all-start.4 = ((bf16[1,2,1440,360]{3,2,0,1:T(8,128)(2,1)}), bf16[1,2,1440,360]{3,2,0,1:T(8,128)(2,1)}, u32[]{:S(2)}, u32[]{:S(2)}) async-start(bf16[1,2,1440,360]{3,2,0,1:T(8,128)(2,1)} %bitcast.134), calls=%async_computation.4 | async-start | bytes 4423680 | tf_op jit(solution)/shard_map/all_to_all | solution.py:91
  208.9 3.4 fusion.90
  212.3 1.6 copy.159
  213.8 18.3 %all-to-all-done.4 = bf16[1,2,1440,360]{3,2,0,1:T(8,128)(2,1)} async-done(((bf16[1,2,1440,360]{3,2,0,1:T(8,128)(2,1)}), bf16[1,2,1440,360]{3,2,0,1:T(8,128)(2,1)}, u32[]{:S(2)}, u32[]{:S(2)}) %all-to-all-start.4) | async-done | bytes 2073632 | tf_op jit(solution)/shard_map/all_to_all | solution.py:91
  232.1 5.2 %all-to-all-start.2 = ((bf16[1,2,1440,360]{3,2,0,1:T(8,128)(2,1)}), bf16[1,2,1440,360]{3,2,0,1:T(8,128)(2,1)}, u32[]{:S(2)}, u32[]{:S(2)}) async-start(bf16[1,2,1440,360]{3,2,0,1:T(8,128)(2,1)} %bitcast.133), calls=%async_computation.2 | async-start | bytes 4423680 | tf_op jit(solution)/shard_map/all_to_all | solution.py:84
  237.4 1.5 fusion.88
  239.1 18.3 %all-reduce.5.cloned.1.call-done = (f32[16,1440]{1,0:T(8,128)}, f32[16,1440]{1,0:T(8,128)}) async-done(((f32[16,1440]{1,0:T(8,128)}, f32[16,1440]{1,0:T(8,128)}), (f32[16,1440]{1,0:T(8,128)}, f32[16,1440]{1,0:T(8,128)})) %all-reduce.5.cloned.1.call-update) | async-done | bytes 184336 | tf_op jit(solution)/shard_map/psum | solution.py:116
  261.1 4.5 %all-to-all-start.8 = ((bf16[8,16,1440]{2,1,0:T(8,128)(2,1)}), bf16[8,16,1440]{2,1,0:T(8,128)(2,1)S(1)}, u32[]{:S(2)}, u32[]{:S(2)}) async-start(bf16[8,16,1440]{2,1,0:T(8,128)(2,1)} %bitcast.38), calls=%async_computation.8 | async-start | bytes 786432 | tf_op jit(solution)/shard_map/all_to_all | solution.py:136
  266.9 2.8 copy.167
  269.7 4.2 %copy.164 = bf16[1,2,1440,360]{2,3,1,0:T(8,128)(2,1)} copy(bf16[1,2,1440,360]{3,2,0,1:T(8,128)(2,1)} %all-to-all-done.4) | data formatting | bytes 4147200 | tf_op jit(solution)/shard_map/all_to_all | solution.py:91
  273.9 2.9 copy.161
  277.7 5.2 %all-to-all-start = ((bf16[8,16,1440]{2,1,0:T(8,128)(2,1)}), bf16[8,16,1440]{2,1,0:T(8,128)(2,1)S(1)}, u32[]{:S(2)}, u32[]{:S(2)}) async-start(bf16[8,16,1440]{2,1,0:T(8,128)(2,1)} %bitcast.4), calls=%async_computation | async-start | bytes 786432 | tf_op jit(solution)/shard_map/all_to_all | solution.py:136
  282.9 1.5 fusion.91
  284.4 5.7 %fusion.4 = f32[128,1440]{0,1:T(8,128)} fusion(bf16[1440,720]{0,1:T(8,128)(2,1)} %bitcast.139, bf16[128,1440]{1,0:T(8,128)(2,1)S(1)} %bitcast.146, bf16[1440,720]{0,1:T(8,128)(2,1)} %bitcast.141, f32[128,720]{0,1:T(8,128)} %fusion.91), kind=kOutput, calls=%fused_computation.10 | convolution fusion | flops 531394560 | bytes 5621760 | tf_op jit(solution)/shard_map/dot_general | solution.py:147
  290.1 4.4 %all-to-all-done = bf16[8,16,1440]{2,1,0:T(8,128)(2,1)S(1)} async-done(((bf16[8,16,1440]{2,1,0:T(8,128)(2,1)}), bf16[8,16,1440]{2,1,0:T(8,128)(2,1)S(1)}, u32[]{:S(2)}, u32[]{:S(2)}) %all-to-all-start) | async-done | bytes 368672 | tf_op jit(solution)/shard_map/all_to_all | solution.py:136
  295.3 4.8 %fusion.5 = f32[128,1440]{0,1:T(8,128)S(1)} fusion(bf16[1440,720]{0,1:T(8,128)(2,1)} %bitcast.140, bf16[128,1440]{1,0:T(8,128)(2,1)S(1)} %bitcast.148, bf16[1440,720]{0,1:T(8,128)(2,1)} %bitcast.142, f32[128,720]{0,1:T(8,128)S(1)} %fusion.89), kind=kOutput, calls=%fused_computation.11 | convolution fusion | flops 531394560 | bytes 5621760 | tf_op jit(solution)/shard_map/dot_general | solution.py:147
  300.1 7.2 %all-reduce.6 = (bf16[128,1440]{0,1:T(8,128)(2,1)S(1)}, bf16[128,1440]{0,1:T(8,128)(2,1)S(1)}) all-reduce(f32[128,1440]{0,1:T(8,128)S(1)} %copy-done.6, f32[128,1440]{0,1:T(8,128)S(1)} %fusion.5), channel_id=1, replica_groups=mesh['groups'=2,'expert'=4,'dp'=2,'tensor'=2] {'tensor'}, use_global_device_ids=true, to_apply=%region_18.19 | all-reduce | flops 368640 | bytes 2211840 | tf_op jit(solution)/shard_map/psum | solution.py:150
  308.2 3.6 %all-to-all-start.9 = ((bf16[8,16,1440]{2,1,0:T(8,128)(2,1)}), bf16[8,16,1440]{2,1,0:T(8,128)(2,1)S(1)}, u32[]{:S(2)}, u32[]{:S(2)}) async-start(bf16[8,16,1440]{2,1,0:T(8,128)(2,1)} %bitcast.46), calls=%async_computation.9 | async-start | bytes 786432 | tf_op jit(solution)/shard_map/all_to_all | solution.py:152
  312.8 11.3 %all-to-all-done.9 = bf16[8,16,1440]{2,1,0:T(8,128)(2,1)S(1)} async-done(((bf16[8,16,1440]{2,1,0:T(8,128)(2,1)}), bf16[8,16,1440]{2,1,0:T(8,128)(2,1)S(1)}, u32[]{:S(2)}, u32[]{:S(2)}) %all-to-all-start.9) | async-done | bytes 368672 | tf_op jit(solution)/shard_map/all_to_all | solution.py:152
  324.1 3.6 %all-to-all-start.7 = ((bf16[8,16,1440]{2,1,0:T(8,128)(2,1)}), bf16[8,16,1440]{2,1,0:T(8,128)(2,1)S(1)}, u32[]{:S(2)}, u32[]{:S(2)}) async-start(bf16[8,16,1440]{2,1,0:T(8,128)(2,1)} %bitcast.30), calls=%async_computation.7 | async-start | bytes 786432 | tf_op jit(solution)/shard_map/all_to_all | solution.py:152
  328.1 11.5 %all-to-all-done.7 = bf16[8,16,1440]{2,1,0:T(8,128)(2,1)S(1)} async-done(((bf16[8,16,1440]{2,1,0:T(8,128)(2,1)}), bf16[8,16,1440]{2,1,0:T(8,128)(2,1)S(1)}, u32[]{:S(2)}, u32[]{:S(2)}) %all-to-all-start.7) | async-done | bytes 368672 | tf_op jit(solution)/shard_map/all_to_all | solution.py:152
  (116 shorter events, 23.0 us)
Async XLA Ops:
  6.5 57.2 %copy-start.5 = (bf16[8,360,360]{2,1,0:T(8,128)(2,1)S(1)}, bf16[8,360,360]{2,1,0:T(8,128)(2,1)}, u32[]{:S(2)}) copy-start(bf16[8,360,360]{2,1,0:T(8,128)(2,1)} %param.26) | copy-start | bytes 6220804
  116.8 4.5 %copy-start.17 = (s32[2,16,4]{1,2,0:T(4,128)S(1)}, s32[2,16,4]{1,2,0:T(4,128)}, u32[]{:S(2)}) copy-start(s32[2,16,4]{1,2,0:T(4,128)} %param.21) | copy-start | bytes 1540
  116.8 6.5 %copy-start.15 = (bf16[2,16,1024]{2,1,0:T(8,128)(2,1)S(1)}, bf16[2,16,1024]{2,1,0:T(8,128)(2,1)}, u32[]{:S(2)}) copy-start(bf16[2,16,1024]{2,1,0:T(8,128)(2,1)} %param.15) | copy-start | bytes 196612
  116.8 7.8 %copy-start.9 = (bf16[16,64,128]{2,1,0:T(8,128)(2,1)S(1)}, bf16[16,64,128]{2,1,0:T(8,128)(2,1)}, u32[]{:S(2)}) copy-start(bf16[16,64,128]{2,1,0:T(8,128)(2,1)} %param.18) | copy-start | bytes 786436
  116.8 53.6 %all-to-all-start.1 = ((bf16[4,2,360,360]{3,2,1,0:T(8,128)(2,1)}), bf16[4,2,360,360]{3,2,1,0:T(8,128)(2,1)S(1)}, u32[]{:S(2)}, u32[]{:S(2)}) async-start(bf16[4,2,360,360]{3,2,1,0:T(8,128)(2,1)} %bitcast.138), calls=%async_computation.1 | async-start | bytes 4423680 | tf_op jit(solution)/shard_map/all_to_all | solution.py:85
  120.5 4.3 %copy-start.20 = (bf16[2,16,128]{2,1,0:T(8,128)(2,1)S(1)}, bf16[2,16,128]{2,1,0:T(8,128)(2,1)}, u32[]{:S(2)}) copy-start(bf16[2,16,128]{2,1,0:T(8,128)(2,1)} %param.16) | copy-start | bytes 24580
  120.6 4.4 %copy-start.21 = (bf16[2,16,128]{2,1,0:T(8,128)(2,1)S(1)}, bf16[2,16,128]{2,1,0:T(8,128)(2,1)}, u32[]{:S(2)}) copy-start(bf16[2,16,128]{2,1,0:T(8,128)(2,1)} %param.17) | copy-start | bytes 24580
  120.6 4.5 %copy-start.10 = (bf16[16,64,128]{2,1,0:T(8,128)(2,1)S(1)}, bf16[16,64,128]{2,1,0:T(8,128)(2,1)}, u32[]{:S(2)}) copy-start(bf16[16,64,128]{2,1,0:T(8,128)(2,1)} %param.19) | copy-start | bytes 786436
  120.6 88.3 %all-gather.2.cloned.1.call-start = ((), (), s32[]{:S(2)}) async-start(), calls=%async_computation.10 | async-start | bytes 4423680 | tf_op jit(solution)/shard_map/all_gather | solution.py:107
  125.0 5.0 %copy-start.19 = (bf16[2,16,2,64]{3,2,1,0:T(2,128)(2,1)}, bf16[2,16,2,64]{3,2,1,0:T(2,128)(2,1)S(1)}, u32[]{:S(2)}) copy-start(bf16[2,16,2,64]{3,2,1,0:T(2,128)(2,1)S(1)} %reshape.349) | copy-start | bytes 24580
  126.2 3.8 %copy-start.11 = (bf16[16,2,8,64]{3,2,1,0:T(8,128)(2,1)}, bf16[16,2,8,64]{3,2,1,0:T(8,128)(2,1)S(1)}, u32[]{:S(2)}) copy-start(bf16[16,2,8,64]{3,2,1,0:T(8,128)(2,1)S(1)} %reshape_squeeze.12) | copy-start | bytes 98308
  170.4 5.2 %copy-start.13 = (s32[64,8]{1,0:T(8,128)S(1)}, s32[64,8]{1,0:T(8,128)}, u32[]{:S(2)}) copy-start(s32[64,8]{1,0:T(8,128)} %reduce_window_sum.17) | copy-start | bytes 6148
  170.4 5.2 %copy-start.25 = (s32[64]{0:T(128)S(1)}, s32[64]{0:T(128)}, u32[]{:S(2)}) copy-start(s32[64]{0:T(128)} %copy-done.24) | copy-start | bytes 772
  170.4 5.4 %copy-start.8 = (f32[16,2,8,2]{3,2,1,0:T(8,128)S(1)}, f32[16,2,8,2]{3,2,1,0:T(8,128)}, u32[]{:S(2)}) copy-start(f32[16,2,8,2]{3,2,1,0:T(8,128)} %get-tuple-element.26) | copy-start | bytes 6148
  170.4 5.7 %copy-start.7 = (f32[16,2,8,2]{3,2,1,0:T(8,128)S(1)}, f32[16,2,8,2]{3,2,1,0:T(8,128)}, u32[]{:S(2)}) copy-start(f32[16,2,8,2]{3,2,1,0:T(8,128)} %get-tuple-element.30) | copy-start | bytes 6148
  171.8 29.3 %all-to-all-start.6 = ((bf16[1,2,1440,360]{3,2,0,1:T(8,128)(2,1)}), bf16[1,2,1440,360]{3,2,0,1:T(8,128)(2,1)S(1)}, u32[]{:S(2)}, u32[]{:S(2)}) async-start(bf16[1,2,1440,360]{3,2,0,1:T(8,128)(2,1)} %bitcast.135), calls=%async_computation.6 | async-start | bytes 4423680 | tf_op jit(solution)/shard_map/all_to_all | solution.py:98
  201.1 6.3 %copy-start.12 = (s32[64,8]{1,0:T(8,128)S(1)}, s32[64,8]{1,0:T(8,128)}, u32[]{:S(2)}) copy-start(s32[64,8]{1,0:T(8,128)} %reduce_window_sum.18) | copy-start | bytes 6148
  201.1 6.3 %copy-start.23 = (s32[64]{0:T(128)S(1)}, s32[64]{0:T(128)}, u32[]{:S(2)}) copy-start(s32[64]{0:T(128)} %copy-done.22) | copy-start | bytes 772
  202.5 29.6 %all-to-all-start.4 = ((bf16[1,2,1440,360]{3,2,0,1:T(8,128)(2,1)}), bf16[1,2,1440,360]{3,2,0,1:T(8,128)(2,1)}, u32[]{:S(2)}, u32[]{:S(2)}) async-start(bf16[1,2,1440,360]{3,2,0,1:T(8,128)(2,1)} %bitcast.134), calls=%async_computation.4 | async-start | bytes 4423680 | tf_op jit(solution)/shard_map/all_to_all | solution.py:91
  208.1 4.2 %copy-start.4 = (bf16[4,2,360,360]{3,2,1,0:T(8,128)(2,1)S(1)}, bf16[4,2,360,360]{3,2,1,0:T(8,128)(2,1)}, u32[]{:S(2)}) copy-start(bf16[4,2,360,360]{3,2,1,0:T(8,128)(2,1)} %copy-done.3) | copy-start | bytes 6220804
  232.1 5.2 %copy-start = (bf16[1024,1440]{0,1:T(8,128)(2,1)S(1)}, bf16[1024,1440]{0,1:T(8,128)(2,1)}, u32[]{:S(2)}) copy-start(bf16[1024,1440]{0,1:T(8,128)(2,1)} %all-gather.2.cloned.1.call-done) | copy-start | bytes 8847364
  232.1 28.9 %all-to-all-start.2 = ((bf16[1,2,1440,360]{3,2,0,1:T(8,128)(2,1)}), bf16[1,2,1440,360]{3,2,0,1:T(8,128)(2,1)}, u32[]{:S(2)}, u32[]{:S(2)}) async-start(bf16[1,2,1440,360]{3,2,0,1:T(8,128)(2,1)} %bitcast.133), calls=%async_computation.2 | async-start | bytes 4423680 | tf_op jit(solution)/shard_map/all_to_all | solution.py:84
  237.3 20.1 %copy-start.14 = (bf16[2,16,1440]{2,1,0:T(8,128)(2,1)S(1)}, bf16[2,16,1440]{2,1,0:T(8,128)(2,1)}, u32[]{:S(2)}) copy-start(bf16[2,16,1440]{2,1,0:T(8,128)(2,1)} %param.14) | copy-start | bytes 276484
  237.3 21.2 %copy-start.16 = (f32[1440]{0:T(1024)S(1)}, f32[1440]{0:T(1024)}, u32[]{:S(2)}) copy-start(f32[1440]{0:T(1024)} %param.23) | copy-start | bytes 17284
  237.3 20.1 %all-reduce.5.cloned.1.call-start = ((), (), s32[]{:S(2)}) async-start(), calls=%async_computation.11 | async-start | bytes 393216 | tf_op jit(solution)/shard_map/psum | solution.py:116
  238.9 28.0 %copy-start.2 = (bf16[1,2,1440,360]{3,2,0,1:T(8,128)(2,1)S(1)}, bf16[1,2,1440,360]{3,2,0,1:T(8,128)(2,1)}, u32[]{:S(2)}) copy-start(bf16[1,2,1440,360]{3,2,0,1:T(8,128)(2,1)} %copy-done.1) | copy-start | bytes 6220804
  261.1 16.6 %all-to-all-start.8 = ((bf16[8,16,1440]{2,1,0:T(8,128)(2,1)}), bf16[8,16,1440]{2,1,0:T(8,128)(2,1)S(1)}, u32[]{:S(2)}, u32[]{:S(2)}) async-start(bf16[8,16,1440]{2,1,0:T(8,128)(2,1)} %bitcast.38), calls=%async_computation.8 | async-start | bytes 786432 | tf_op jit(solution)/shard_map/all_to_all | solution.py:136
  277.7 16.8 %all-to-all-start = ((bf16[8,16,1440]{2,1,0:T(8,128)(2,1)}), bf16[8,16,1440]{2,1,0:T(8,128)(2,1)S(1)}, u32[]{:S(2)}, u32[]{:S(2)}) async-start(bf16[8,16,1440]{2,1,0:T(8,128)(2,1)} %bitcast.4), calls=%async_computation | async-start | bytes 786432 | tf_op jit(solution)/shard_map/all_to_all | solution.py:136
  295.3 4.8 %copy-start.6 = (f32[128,1440]{0,1:T(8,128)S(1)}, f32[128,1440]{0,1:T(8,128)}, u32[]{:S(2)}) copy-start(f32[128,1440]{0,1:T(8,128)} %fusion.4) | copy-start | bytes 2211844
  300.1 27.6 %copy-start.26 = (f32[2,16,4]{1,2,0:T(4,128)S(1)}, f32[2,16,4]{1,2,0:T(4,128)}, u32[]{:S(2)}) copy-start(f32[2,16,4]{1,2,0:T(4,128)} %param.22) | copy-start | bytes 1540
  308.2 15.9 %all-to-all-start.9 = ((bf16[8,16,1440]{2,1,0:T(8,128)(2,1)}), bf16[8,16,1440]{2,1,0:T(8,128)(2,1)S(1)}, u32[]{:S(2)}, u32[]{:S(2)}) async-start(bf16[8,16,1440]{2,1,0:T(8,128)(2,1)} %bitcast.46), calls=%async_computation.9 | async-start | bytes 786432 | tf_op jit(solution)/shard_map/all_to_all | solution.py:152
  324.1 15.5 %all-to-all-start.7 = ((bf16[8,16,1440]{2,1,0:T(8,128)(2,1)}), bf16[8,16,1440]{2,1,0:T(8,128)(2,1)S(1)}, u32[]{:S(2)}, u32[]{:S(2)}) async-start(bf16[8,16,1440]{2,1,0:T(8,128)(2,1)} %bitcast.30), calls=%async_computation.7 | async-start | bytes 786432 | tf_op jit(solution)/shard_map/all_to_all | solution.py:152
  (5 other events, 11.1 us)
Sparse Core Ops, SparseCore 0:
  123.0 44.1 all-gather.1
  240.5 16.8 all-reduce.4
where the time goes:
time: 349 us; the launch traced here: 347 us
  waiting for transfers between devices  122 us (35%)
  blocking collectives  117 us (34%)
  starting transfers between devices  34.6 us (10%)
  local copies, waits for them, and re-layouts  28.6 us (8%)
  matrix products  25.6 us (7%)
  between operations  13.9 us (4%)
  other arithmetic  5.52 us (2%)
    all_to_all x1, blocking collectives, local(): lax.all_to_all(doubled[2], 'expert', split_axis=0, concat_axis=2, tiled=T...  57.2 us
    all_to_all x1, blocking collectives, local(): lax.all_to_all(doubled[1], 'expert', split_axis=0, concat_axis=2, tiled=T...  53 us
    all_to_all x1, waiting for transfers between devices, local(): lax.all_to_all(doubled[0], 'expert', split_axis=0, concat_axis=2, tiled=T...  34.2 us
    all_to_all x2, waiting for transfers between devices, local(): lax.all_to_all(expert_out.reshape(expert_count * row_count, slot_count, o...  22.8 us
    all_to_all x1, waiting for transfers between devices, local(): lax.all_to_all(lax.all_to_all(doubled[2], 'expert', split_axis=0, concat_...  20.8 us
    psum x1, waiting for transfers between devices, local(): lax.psum(partial_value, 'tensor')  18.3 us
    all_to_all x1, waiting for transfers between devices, local(): lax.all_to_all(lax.all_to_all(doubled[1], 'expert', split_axis=0, concat_...  18.3 us
    dot_general x2, matrix products, local(): lax.dot_general(activated, down_w, (((1,), (1,)), ((), ())), preferred_el...  10.5 us
  transfers between devices with their start and end apart: 10, of which 9 were waited for; matrix products, arithmetic and copies ran while one was open for 14% of the time, Pallas kernels for 0%

commit v1 on v0

--- a/solution.py
+++ b/solution.py
@@ -44,7 +44,7 @@
     return attended.reshape(batch_size, groups * per_group * HEAD_DIM).astype(jnp.bfloat16)
 
 
-def local(
+def move_weights(
     x_res,
     query_new,
     key_new,
@@ -172,6 +172,141 @@
     return jnp.stack(results)
 
 
+def attend_steps(query_new, key_cache, value_cache, key_new, value_new, lengths):
+    steps, batch_size, query_width = query_new.shape
+    groups = key_cache.shape[2] // HEAD_DIM
+    per_group = query_width // (groups * HEAD_DIM)
+    window = key_cache.shape[1]
+    queries = query_new.reshape(steps, batch_size, groups, per_group, HEAD_DIM)
+    queries = queries.transpose(1, 2, 0, 3, 4).reshape(
+        batch_size, groups, steps * per_group, HEAD_DIM
+    )
+    keys = jnp.concatenate([key_cache, key_new.transpose(1, 0, 2)], axis=1)
+    values = jnp.concatenate([value_cache, value_new.transpose(1, 0, 2)], axis=1)
+    spots = window + steps
+    keys = keys.reshape(batch_size, spots, groups, HEAD_DIM)
+    values = values.reshape(batch_size, spots, groups, HEAD_DIM)
+    scores = jnp.einsum("bgrd,bcgd->bgrc", queries, keys, preferred_element_type=jnp.float32)
+    scores = scores * HEAD_DIM ** (-0.5)
+    spot = jnp.arange(spots)[None, None, None, :]
+    moment = (jnp.arange(steps * per_group) // per_group)[None, None, :, None]
+    limit = lengths[:, None, None, None]
+    valid = (spot < limit) | ((spot >= window) & (spot - window <= moment))
+    scores = jnp.where(valid, scores, -jnp.inf)
+    powers = jnp.exp(scores - jnp.max(scores, axis=-1, keepdims=True))
+    probs = (powers / jnp.sum(powers, axis=-1, keepdims=True)).astype(jnp.bfloat16)
+    attended = jnp.einsum("bgrc,bcgd->bgrd", probs, values, preferred_element_type=jnp.float32)
+    attended = attended.astype(jnp.bfloat16).reshape(
+        batch_size, groups, steps, per_group, HEAD_DIM
+    )
+    return attended.transpose(2, 0, 1, 3, 4).reshape(steps * batch_size, query_width)
+
+
+def move_tokens(
+    x_res,
+    query_new,
+    key_new,
+    value_new,
+    key_cache,
+    value_cache,
+    lengths,
+    routes,
+    route_weight,
+    norm_gain,
+    out_weight,
+    w_gate,
+    w_up,
+    w_down,
+):
+    slices = lax.axis_size("expert")
+    rows = lax.axis_size("dp")
+    halves = lax.axis_size("tensor")
+    experts, row_part, col_part = w_gate.shape
+    steps, tokens, width = x_res.shape
+    top = routes.shape[2]
+    mine = steps * tokens
+    block = mine // halves
+    whole = mine * slices * rows
+    everyone = ("expert", "dp", "tensor")
+
+    packed = jnp.concatenate([routes.astype(jnp.float32), route_weight], axis=2)
+    packed = lax.all_gather(packed.reshape(mine, 2 * top), ("expert", "dp"), axis=0, tiled=True)
+    chosen = packed[:, :top].astype(jnp.int32)
+    weight = packed[:, top:]
+
+    attended = attend_steps(query_new, key_cache, value_cache, key_new, value_new, lengths)
+    both = lax.all_gather(attended, "dp", axis=0, tiled=True)
+    partial = jnp.dot(both, out_weight, preferred_element_type=jnp.float32)
+    partial = lax.all_to_all(
+        partial.reshape(rows * halves, block, -1),
+        ("dp", "tensor"),
+        split_axis=0,
+        concat_axis=0,
+        tiled=True,
+    )
+    projected = jnp.sum(partial.reshape(rows, halves, block, -1), axis=1)
+    projected = projected.transpose(1, 0, 2).reshape(block, width)
+    half = lax.axis_index("tensor")
+    own = lax.dynamic_slice_in_dim(x_res.reshape(mine, width), half * block, block, 0)
+    hidden_state = own.astype(jnp.float32) + projected
+    mean_square = jnp.mean(hidden_state * hidden_state, axis=-1, keepdims=True)
+    normed = (hidden_state * lax.rsqrt(mean_square + 1e-05) * norm_gain).astype(jnp.bfloat16)
+
+    normed = lax.all_gather(normed, everyone, axis=0, tiled=True)
+    place = lax.axis_index("expert")
+    features = lax.dynamic_slice_in_dim(normed, place * row_part, row_part, 1)
+    sums = []
+    for matrix in (w_gate, w_up):
+        dense = [
+            jnp.dot(features, matrix[x], preferred_element_type=jnp.float32).astype(jnp.bfloat16)
+            for x in range(experts)
+        ]
+        for k in range(top):
+            value = dense[0]
+            for x in range(1, experts):
+                value = jnp.where(chosen[:, k : k + 1] == x, dense[x], value)
+            sums.append(value.reshape(slices, whole // slices, col_part))
+    sums = jnp.stack(sums, axis=1)
+    sums = lax.psum_scatter(sums, "expert", scatter_dimension=0, tiled=True)[0]
+    sums = sums.astype(jnp.float32)
+    share = lax.dynamic_slice_in_dim(weight, place * (whole // slices), whole // slices, 0)
+    activated = jax.nn.silu(sums[:top]) * sums[top:] * share.T[:, :, None]
+    activated = lax.all_gather(activated.astype(jnp.bfloat16), "expert", axis=0)
+    total = jnp.zeros((whole, row_part), jnp.float32)
+    for x in range(experts):
+        spread = jnp.zeros((whole, col_part), jnp.bfloat16)
+        for k in range(top):
+            spread = jnp.where(
+                chosen[:, k : k + 1] == x, activated[:, k].reshape(whole, col_part), spread
+            )
+        total = total + lax.dot_general(
+            spread, w_down[x], (((1,), (1,)), ((), ())), preferred_element_type=jnp.float32
+        )
+    returned = lax.all_to_all(
+        total.reshape(slices * rows * halves, block, row_part),
+        everyone,
+        split_axis=0,
+        concat_axis=0,
+        tiled=True,
+    )
+    combined = jnp.sum(returned.reshape(slices, rows * halves, block, row_part), axis=1)
+    combined = combined.transpose(1, 0, 2).reshape(block, width)
+    result = (hidden_state + combined).astype(jnp.bfloat16).reshape(block, halves, width // halves)
+    result = lax.all_to_all(
+        result.transpose(1, 0, 2), "tensor", split_axis=0, concat_axis=0, tiled=True
+    )
+    return result.reshape(steps, tokens, width // halves)
+
+
+def local(*args):
+    x_res, routes, w_gate = args[0], args[7], args[11]
+    spread = lax.axis_size("expert") * lax.axis_size("dp")
+    travelling = x_res.shape[0] * x_res.shape[1] * spread * routes.shape[2]
+    if travelling < w_gate.shape[0] * w_gate.shape[1]:
+        return move_tokens(*args)
+    return move_weights(*args)
+
+
 def solution(mesh):
     in_specs = (
         P(None, ("groups", "expert", "dp"), None),

time: 349 us -> 221 us (0.63)
  waiting for transfers between devices: 122 us -> 44.4 us
  starting transfers between devices: 34.6 us -> 3.41 us
  blocking collectives: 117 us -> 99 us
  matrix products: 25.6 us -> 13 us
  local copies, waits for them, and re-layouts: 28.6 us -> 38.3 us
    all_to_all x8 -> x1, waiting for transfers between devices: 103 us -> 0.01 us  [move_tokens(): lax.all_to_all(partial.reshape(rows * halves, block, -1), ('dp', 'tensor'...]
    all_to_all x2, blocking collectives: 110 us -> 19.6 us  [the longest x1 15.9 us: move_tokens(): lax.all_to_all(total.reshape(slices * rows * halves, block, row_part), ev...]
    all_gather x0 -> x4, blocking collectives: none -> 79.4 us  [the longest x1 31.3 us: move_tokens(): lax.all_gather(packed.reshape(mine, 2 * top), ('expert', 'dp'), axis=0, t...]
    unnamed x2, waiting for transfers between devices: 0.7 us -> 44.4 us
    all_to_all x8 -> x1, starting transfers between devices: 34.5 us -> 3.36 us  [move_tokens(): lax.all_to_all(partial.reshape(rows * halves, block, -1), ('dp', 'tensor'...]
    broadcast_in_dim x0 -> x32, local copies, waits for them, and re-layouts: none -> 20.9 us  [the longest x28 18 us: move_tokens(): value = jnp.where(chosen[:, k:k + 1] == x, dense[x], value)]
    psum x1 -> x0, waiting for transfers between devices: 18.3 us -> none  [local(): lax.psum(partial_value, 'tensor')]
    all_to_all x6 -> x0, local copies, waits for them, and re-layouts: 18.2 us -> none  [the longest x1 4.21 us: local(): lax.all_to_all(lax.all_to_all(doubled[1], 'expert', split_axis=0, concat_...]
  transfers between devices with their start and end apart: 10 -> 2, of which waited for: 9 -> 1; matrix products, arithmetic and copies ran while one was open for 14% -> 10% of each run, Pallas kernels for 0% -> 0%
where the time goes in v1:
time: 221 us; the launch traced here: 220 us
  blocking collectives  99 us (45%)
  waiting for transfers between devices  44.4 us (20%)
  local copies, waits for them, and re-layouts  38.3 us (17%)
  between operations  14.3 us (6%)
  matrix products  13 us (6%)
  other arithmetic  7.9 us (4%)
  starting transfers between devices  3.41 us (2%)
    unnamed x2, waiting for transfers between devices  44.4 us
    all_gather x1, blocking collectives, move_tokens(): lax.all_gather(packed.reshape(mine, 2 * top), ('expert', 'dp'), axis=0, t...  31.3 us
    all_gather x1, blocking collectives, move_tokens(): normed = lax.all_gather(normed, everyone, axis=0, tiled=True)  24.3 us
    broadcast_in_dim x28, local copies, waits for them, and re-layouts, move_tokens(): value = jnp.where(chosen[:, k:k + 1] == x, dense[x], value)  18 us
    all_gather x1, blocking collectives, move_tokens(): activated = lax.all_gather(activated.astype(jnp.bfloat16), 'expert', axis=0)  18 us
    all_to_all x1, blocking collectives, move_tokens(): lax.all_to_all(total.reshape(slices * rows * halves, block, row_part), ev...  15.9 us
    unnamed x87, local copies, waits for them, and re-layouts  9.71 us
    dot_general x16, matrix products, move_tokens(): jnp.dot(features, matrix[x], preferred_element_type=jnp.float32)  8.19 us
  transfers between devices with their start and end apart: 2, of which 1 were waited for; matrix products, arithmetic and copies ran while one was open for 10% of the time, Pallas kernels for 0%

profile of v1, /device:TPU:0, one launch (start us, length us, event | category | flops | bytes accessed | tf_op | source)
XLA Modules:
  0.0 220.4 jit_solution(9379384033411356024)
XLA Ops:
  6.6 0.8 copy.129
  8.1 1.0 reshape.394
  9.1 1.0 pad_maximum_fusion.1
  10.4 1.0 pad_maximum_fusion
  12.3 0.9 fusion.5
  13.4 5.8 %all_gather.15 = bf16[64,1024]{1,0:T(8,128)(2,1)S(1)} all-gather(bf16[32,1024]{1,0:T(8,128)(2,1)S(1)} %reshape.398), channel_id=1, replica_groups=mesh['groups'=2,'expert'=4,'dp'=2,'tensor'=2] {'dp'}, dimensions={0}, use_global_device_ids=true | all-gather | bytes 196608 | tf_op jit(solution)/shard_map/all_gather | solution.py:238
  19.3 1.2 fusion.65
  20.5 3.4 %all-to-all-start = ((f32[4,16,720]{2,1,0:T(8,128)}), f32[4,16,720]{2,1,0:T(8,128)S(1)}, u32[]{:S(2)}, u32[]{:S(2)}) async-start(f32[4,16,720]{2,1,0:T(8,128)} %bitcast.10), calls=%async_computation | async-start | bytes 393216 | tf_op jit(solution)/shard_map/all_to_all | solution.py:240
  24.1 31.3 %all-gather.1 = f32[8,32,8]{1,2,0:T(8,128)S(1)} all-gather(f32[1,32,8]{1,2,0:T(8,128)S(1)} %reshape.408), channel_id=1, replica_groups=mesh['groups'=2,'expert'=4,'dp'=2,'tensor'=2] {'expert','dp'}, dimensions={0}, use_global_device_ids=true | all-gather | bytes 9216 | tf_op jit(solution)/shard_map/all_gather | solution.py:233
  56.9 24.3 %all_gather.17 = bf16[256,1440]{1,0:T(8,128)(2,1)S(1)} all-gather(bf16[16,1440]{1,0:T(8,128)(2,1)S(1)} %multiply_convert_fusion), channel_id=1, replica_groups=mesh['groups'=2,'expert'=4,'dp'=2,'tensor'=2] {'expert','dp','tensor'}, dimensions={0}, use_global_device_ids=true | all-gather | bytes 783360 | tf_op jit(solution)/shard_map/all_gather | solution.py:255
  81.1 1.5 convolution_convert_fusion.14
  82.6 1.3 convolution_convert_fusion.13
  90.5 0.8 copy.98
  91.5 0.8 copy.100
  92.3 0.8 copy.105
  93.1 0.8 copy.103
  93.9 0.8 copy.99
  94.7 0.8 copy.101
  95.5 1.0 constant_dynamic-update-slice_fusion.7
  96.5 1.0 constant_dynamic-update-slice_fusion.6
  97.5 1.0 constant_dynamic-update-slice_fusion.5
  98.5 1.0 constant_dynamic-update-slice_fusion.4
  99.5 1.0 constant_dynamic-update-slice_fusion.2
  100.5 1.1 copy-done.2
  105.1 0.8 broadcast_in_dim.619
  121.8 0.8 broadcast_in_dim.591
  122.6 1.2 dynamic-slice
  123.9 44.4 %all-reduce.3.cloned.1.call-done = bf16[4,8,64,360]{3,2,0,1:T(8,128)(2,1)} async-done(((bf16[4,8,64,360]{3,2,0,1:T(8,128)(2,1)}), bf16[4,8,64,360]{3,2,0,1:T(8,128)(2,1)}) %all-reduce.3.cloned.1.call-update) | async-done | bytes 1474576
  168.3 1.9 fusion.58
  170.4 18.0 %all-gather = bf16[16,64,360]{2,1,0:T(8,128)(2,1)S(1)} all-gather(bf16[4,64,360]{2,1,0:T(8,128)(2,1)S(1)} %fusion.8), channel_id=2, replica_groups=mesh['groups'=2,'expert'=4,'dp'=2,'tensor'=2] {'expert'}, dimensions={0}, use_global_device_ids=true | all-gather | bytes 921600 | tf_op jit(solution)/shard_map/all_gather | solution.py:274
  192.9 15.9 %all_to_all.15 = f32[16,16,360]{2,1,0:T(8,128)S(1)} all-to-all(f32[16,16,360]{2,1,0:T(8,128)S(1)} %bitcast.247), channel_id=1, replica_groups=mesh['groups'=2,'expert'=4,'dp'=2,'tensor'=2] {'expert','dp','tensor'}, dimensions={0} | all-to-all | bytes 737280 | tf_op jit(solution)/shard_map/all_to_all | solution.py:285
  209.1 3.8 %all_to_all.16 = bf16[2,16,720]{2,1,0:T(8,128)(2,1)S(1)} all-to-all(bf16[2,16,720]{2,1,0:T(8,128)(2,1)S(1)} %copy.113), channel_id=1, replica_groups=mesh['groups'=2,'expert'=4,'dp'=2,'tensor'=2] {'tensor'}, dimensions={0} | all-to-all | bytes 92160 | tf_op jit(solution)/shard_map/all_to_all | solution.py:295
  (179 shorter events, 35.0 us)
Async XLA Ops:
  13.2 43.4 %copy-start.6 = (bf16[2,16,1440]{2,1,0:T(8,128)(2,1)S(1)}, bf16[2,16,1440]{2,1,0:T(8,128)(2,1)}, u32[]{:S(2)}) copy-start(bf16[2,16,1440]{2,1,0:T(8,128)(2,1)} %param.14) | copy-start | bytes 276484
  13.2 43.5 %copy-start.8 = (f32[1440]{0:T(1024)S(1)}, f32[1440]{0:T(1024)}, u32[]{:S(2)}) copy-start(f32[1440]{0:T(1024)} %param.23) | copy-start | bytes 17284
  20.5 35.9 %all-to-all-start = ((f32[4,16,720]{2,1,0:T(8,128)}), f32[4,16,720]{2,1,0:T(8,128)S(1)}, u32[]{:S(2)}, u32[]{:S(2)}) async-start(f32[4,16,720]{2,1,0:T(8,128)} %bitcast.10), calls=%async_computation | async-start | bytes 393216 | tf_op jit(solution)/shard_map/all_to_all | solution.py:240
  23.9 144.4 %all-reduce.3.cloned.1.call-start = ((), (), s32[]{:S(2)}) async-start(), calls=%async_computation.3 | async-start | bytes 3145728
  56.1 32.9 %copy-start.30 = (pred[256]{0:T(512)(128)(4,1)}, pred[256]{0:T(512)(128)(4,1)S(1)}, u32[]{:S(2)}) copy-start(pred[256]{0:T(512)(128)(4,1)S(1)} %get-tuple-element.59) | copy-start | bytes 772
  56.1 32.9 %copy-start.31 = (pred[256]{0:T(512)(128)(4,1)}, pred[256]{0:T(512)(128)(4,1)S(1)}, u32[]{:S(2)}) copy-start(pred[256]{0:T(512)(128)(4,1)S(1)} %get-tuple-element.58) | copy-start | bytes 772
  56.2 32.9 %copy-start.32 = (pred[256]{0:T(512)(128)(4,1)}, pred[256]{0:T(512)(128)(4,1)S(1)}, u32[]{:S(2)}) copy-start(pred[256]{0:T(512)(128)(4,1)S(1)} %get-tuple-element.57) | copy-start | bytes 772
  56.2 32.9 %copy-start.33 = (pred[256]{0:T(512)(128)(4,1)}, pred[256]{0:T(512)(128)(4,1)S(1)}, u32[]{:S(2)}) copy-start(pred[256]{0:T(512)(128)(4,1)S(1)} %get-tuple-element.56) | copy-start | bytes 772
  56.2 32.9 %copy-start.34 = (pred[256]{0:T(512)(128)(4,1)}, pred[256]{0:T(512)(128)(4,1)S(1)}, u32[]{:S(2)}) copy-start(pred[256]{0:T(512)(128)(4,1)S(1)} %get-tuple-element.55) | copy-start | bytes 772
  56.2 32.9 %copy-start.35 = (pred[256]{0:T(512)(128)(4,1)}, pred[256]{0:T(512)(128)(4,1)S(1)}, u32[]{:S(2)}) copy-start(pred[256]{0:T(512)(128)(4,1)S(1)} %get-tuple-element.54) | copy-start | bytes 772
  56.2 32.9 %copy-start.36 = (pred[256]{0:T(512)(128)(4,1)}, pred[256]{0:T(512)(128)(4,1)S(1)}, u32[]{:S(2)}) copy-start(pred[256]{0:T(512)(128)(4,1)S(1)} %get-tuple-element.35) | copy-start | bytes 772
  56.2 33.4 %copy-start.18 = (pred[256]{0:T(512)(128)(4,1)}, pred[256]{0:T(512)(128)(4,1)S(1)}, u32[]{:S(2)}) copy-start(pred[256]{0:T(512)(128)(4,1)S(1)} %get-tuple-element.32) | copy-start | bytes 772
  56.2 33.4 %copy-start.19 = (pred[256]{0:T(512)(128)(4,1)}, pred[256]{0:T(512)(128)(4,1)S(1)}, u32[]{:S(2)}) copy-start(pred[256]{0:T(512)(128)(4,1)S(1)} %get-tuple-element.31) | copy-start | bytes 772
  56.2 33.4 %copy-start.20 = (pred[256]{0:T(512)(128)(4,1)}, pred[256]{0:T(512)(128)(4,1)S(1)}, u32[]{:S(2)}) copy-start(pred[256]{0:T(512)(128)(4,1)S(1)} %get-tuple-element.30) | copy-start | bytes 772
  56.2 33.4 %copy-start.21 = (pred[256]{0:T(512)(128)(4,1)}, pred[256]{0:T(512)(128)(4,1)S(1)}, u32[]{:S(2)}) copy-start(pred[256]{0:T(512)(128)(4,1)S(1)} %get-tuple-element.29) | copy-start | bytes 772
  56.2 33.4 %copy-start.22 = (pred[256]{0:T(512)(128)(4,1)}, pred[256]{0:T(512)(128)(4,1)S(1)}, u32[]{:S(2)}) copy-start(pred[256]{0:T(512)(128)(4,1)S(1)} %get-tuple-element.28) | copy-start | bytes 772
  56.2 33.4 %copy-start.23 = (pred[256]{0:T(512)(128)(4,1)}, pred[256]{0:T(512)(128)(4,1)S(1)}, u32[]{:S(2)}) copy-start(pred[256]{0:T(512)(128)(4,1)S(1)} %get-tuple-element.27) | copy-start | bytes 772
  56.2 33.4 %copy-start.26 = (pred[256]{0:T(512)(128)(4,1)}, pred[256]{0:T(512)(128)(4,1)S(1)}, u32[]{:S(2)}) copy-start(pred[256]{0:T(512)(128)(4,1)S(1)} %get-tuple-element.23) | copy-start | bytes 772
  56.3 33.6 %copy-start.9 = (pred[256]{0:T(512)(128)(4,1)}, pred[256]{0:T(512)(128)(4,1)S(1)}, u32[]{:S(2)}) copy-start(pred[256]{0:T(512)(128)(4,1)S(1)} %get-tuple-element.63) | copy-start | bytes 772
  56.3 33.6 %copy-start.10 = (pred[256]{0:T(512)(128)(4,1)}, pred[256]{0:T(512)(128)(4,1)S(1)}, u32[]{:S(2)}) copy-start(pred[256]{0:T(512)(128)(4,1)S(1)} %get-tuple-element.62) | copy-start | bytes 772
  56.3 33.6 %copy-start.11 = (pred[256]{0:T(512)(128)(4,1)}, pred[256]{0:T(512)(128)(4,1)S(1)}, u32[]{:S(2)}) copy-start(pred[256]{0:T(512)(128)(4,1)S(1)} %get-tuple-element.61) | copy-start | bytes 772
  56.3 33.6 %copy-start.12 = (pred[256]{0:T(512)(128)(4,1)}, pred[256]{0:T(512)(128)(4,1)S(1)}, u32[]{:S(2)}) copy-start(pred[256]{0:T(512)(128)(4,1)S(1)} %get-tuple-element.60) | copy-start | bytes 772
  56.3 33.9 %copy-start.13 = (pred[256]{0:T(512)(128)(4,1)}, pred[256]{0:T(512)(128)(4,1)S(1)}, u32[]{:S(2)}) copy-start(pred[256]{0:T(512)(128)(4,1)S(1)} %get-tuple-element.52) | copy-start | bytes 772
  56.3 33.9 %copy-start.14 = (pred[256]{0:T(512)(128)(4,1)}, pred[256]{0:T(512)(128)(4,1)S(1)}, u32[]{:S(2)}) copy-start(pred[256]{0:T(512)(128)(4,1)S(1)} %get-tuple-element.51) | copy-start | bytes 772
  56.3 33.9 %copy-start.15 = (pred[256]{0:T(512)(128)(4,1)}, pred[256]{0:T(512)(128)(4,1)S(1)}, u32[]{:S(2)}) copy-start(pred[256]{0:T(512)(128)(4,1)S(1)} %get-tuple-element.50) | copy-start | bytes 772
  56.3 33.9 %copy-start.16 = (pred[256]{0:T(512)(128)(4,1)}, pred[256]{0:T(512)(128)(4,1)S(1)}, u32[]{:S(2)}) copy-start(pred[256]{0:T(512)(128)(4,1)S(1)} %get-tuple-element.49) | copy-start | bytes 772
  56.3 33.9 %copy-start.17 = (pred[256]{0:T(512)(128)(4,1)}, pred[256]{0:T(512)(128)(4,1)S(1)}, u32[]{:S(2)}) copy-start(pred[256]{0:T(512)(128)(4,1)S(1)} %get-tuple-element.34) | copy-start | bytes 772
  56.3 33.9 %copy-start.24 = (pred[256]{0:T(512)(128)(4,1)}, pred[256]{0:T(512)(128)(4,1)S(1)}, u32[]{:S(2)}) copy-start(pred[256]{0:T(512)(128)(4,1)S(1)} %get-tuple-element.25) | copy-start | bytes 772
  56.4 33.9 %copy-start.25 = (pred[256]{0:T(512)(128)(4,1)}, pred[256]{0:T(512)(128)(4,1)S(1)}, u32[]{:S(2)}) copy-start(pred[256]{0:T(512)(128)(4,1)S(1)} %get-tuple-element.24) | copy-start | bytes 772
  56.6 27.3 %copy-start.4 = (bf16[8,360,360]{2,1,0:T(8,128)(2,1)S(1)}, bf16[8,360,360]{2,1,0:T(8,128)(2,1)}, u32[]{:S(2)}) copy-start(bf16[8,360,360]{2,1,0:T(8,128)(2,1)} %param.25) | copy-start | bytes 6220804
  168.3 20.5 %copy-start.1 = (bf16[8,360,360]{2,1,0:T(8,128)(2,1)S(1)}, bf16[8,360,360]{2,1,0:T(8,128)(2,1)}, u32[]{:S(2)}) copy-start(bf16[8,360,360]{2,1,0:T(8,128)(2,1)} %param.27) | copy-start | bytes 6220804
  192.1 16.9 %copy-start.7 = (bf16[2,16,1440]{2,1,0:T(8,128)(2,1)S(1)}, bf16[2,16,1440]{2,1,0:T(8,128)(2,1)}, u32[]{:S(2)}) copy-start(bf16[2,16,1440]{2,1,0:T(8,128)(2,1)} %param.14) | copy-start | bytes 276484
  (7 other events, 52.0 us)
Sparse Core Ops, SparseCore 0:
  101.8 66.4 all-reduce.2

commit v2 on v0

--- a/solution.py
+++ b/solution.py
@@ -1,6 +1,10 @@
+import functools
+
 import jax
 import jax.numpy as jnp
 from jax import lax
+from jax.experimental import pallas as pl
+from jax.experimental.pallas import tpu as pltpu
 from jax.sharding import PartitionSpec as P
 
 HEAD_DIM = 64
@@ -44,7 +48,7 @@
     return attended.reshape(batch_size, groups * per_group * HEAD_DIM).astype(jnp.bfloat16)
 
 
-def local(
+def move_weights(
     x_res,
     query_new,
     key_new,
@@ -172,6 +176,396 @@
     return jnp.stack(results)
 
 
+def attend_steps(query_new, key_cache, value_cache, key_new, value_new, lengths):
+    steps, batch_size, query_width = query_new.shape
+    groups = key_cache.shape[2] // HEAD_DIM
+    per_group = query_width // (groups * HEAD_DIM)
+    window = key_cache.shape[1]
+    queries = query_new.reshape(steps, batch_size, groups, per_group, HEAD_DIM)
+    queries = queries.transpose(1, 2, 0, 3, 4).reshape(
+        batch_size, groups, steps * per_group, HEAD_DIM
+    )
+    keys = jnp.concatenate([key_cache, key_new.transpose(1, 0, 2)], axis=1)
+    values = jnp.concatenate([value_cache, value_new.transpose(1, 0, 2)], axis=1)
+    spots = window + steps
+    keys = keys.reshape(batch_size, spots, groups, HEAD_DIM)
+    values = values.reshape(batch_size, spots, groups, HEAD_DIM)
+    scores = jnp.einsum("bgrd,bcgd->bgrc", queries, keys, preferred_element_type=jnp.float32)
+    scores = scores * HEAD_DIM ** (-0.5)
+    spot = jnp.arange(spots)[None, None, None, :]
+    moment = (jnp.arange(steps * per_group) // per_group)[None, None, :, None]
+    limit = lengths[:, None, None, None]
+    valid = (spot < limit) | ((spot >= window) & (spot - window <= moment))
+    scores = jnp.where(valid, scores, -jnp.inf)
+    powers = jnp.exp(scores - jnp.max(scores, axis=-1, keepdims=True))
+    probs = (powers / jnp.sum(powers, axis=-1, keepdims=True)).astype(jnp.bfloat16)
+    attended = jnp.einsum("bgrc,bcgd->bgrd", probs, values, preferred_element_type=jnp.float32)
+    attended = attended.astype(jnp.bfloat16).reshape(
+        batch_size, groups, steps, per_group, HEAD_DIM
+    )
+    return attended.transpose(2, 0, 1, 3, 4).reshape(steps * batch_size, query_width)
+
+
+def layer_kernel(
+    slices,
+    rows,
+    halves,
+    top,
+    att_ref,
+    packed_ref,
+    x_ref,
+    gain_ref,
+    out_ref_w,
+    gate_hbm,
+    up_hbm,
+    down_hbm,
+    result_ref,
+    gate_ref,
+    up_ref,
+    down_ref,
+    routing,
+    att_other,
+    proj_out,
+    proj_in,
+    hidden,
+    norm_out,
+    features,
+    sums_out,
+    sums_in,
+    act_all,
+    down_out,
+    down_in,
+    part_out,
+    part_in,
+    final,
+    weight_sem,
+    att_sem,
+    route_sem,
+    proj_sem,
+    norm_sem,
+    sums_sem,
+    act_sem,
+    down_sem,
+    part_sem,
+    swap_sem,
+):
+    f32, bf16 = jnp.float32, jnp.bfloat16
+    z, x, c = lax.axis_index("expert"), lax.axis_index("dp"), lax.axis_index("tensor")
+    quad = rows * halves
+    count = slices * quad
+    here = x * halves + c
+    me = z * quad + here
+    per = out_ref_w.shape[0]
+    block = x_ref.shape[2]
+    part = x_ref.shape[3]
+    experts = gate_ref.shape[0]
+
+    def device(index):
+        return {"expert": index // quad, "dp": (index // halves) % rows, "tensor": index % halves}
+
+    def send(source, target, sems, slot, index):
+        return pltpu.make_async_remote_copy(
+            src_ref=source,
+            dst_ref=target,
+            send_sem=sems.at[0, slot],
+            recv_sem=sems.at[1, slot],
+            device_id=device(index),
+            device_id_type=pl.DeviceIdType.MESH,
+        )
+
+    loads = [
+        pltpu.make_async_copy(source, target, weight_sem.at[i])
+        for i, (source, target) in enumerate(
+            ((gate_hbm, gate_ref), (up_hbm, up_ref), (down_hbm, down_ref))
+        )
+    ]
+    for load in loads:
+        load.start()
+
+    barrier = pltpu.get_barrier_semaphore()
+    for d in range(1, count):
+        pl.semaphore_signal(
+            barrier,
+            inc=1,
+            device_id=device(lax.rem(me + d, count)),
+            device_id_type=pl.DeviceIdType.MESH,
+        )
+    pl.semaphore_wait(barrier, count - 1)
+
+    att_copies = []
+    for d in range(1, rows):
+        peer = z * quad + lax.rem(x + d, rows) * halves + c
+        att_copies.append(send(att_ref, att_other.at[d - 1], att_sem, d, peer))
+        att_copies[-1].start()
+    route_copies = []
+    for d in range(1, count):
+        peer = lax.rem(me + d, count)
+        route_copies.append(send(packed_ref.at[c], routing.at[me], route_sem, d, peer))
+        route_copies[-1].start()
+    routing[me] = packed_ref[c]
+
+    def project(value, owner):
+        for j in range(per):
+            product = jnp.dot(value, out_ref_w[j], preferred_element_type=f32)
+            for h in range(halves):
+                proj_out[owner * halves + h, j] = product[h * block : (h + 1) * block]
+
+    project(att_ref[...], x)
+    for d in range(1, rows):
+        att_copies[d - 1].wait()
+        project(att_other[d - 1], lax.rem(x - d + rows, rows))
+
+    proj_copies = []
+    for d in range(1, quad):
+        spot = lax.rem(here + d, quad)
+        proj_copies.append(
+            send(proj_out.at[spot], proj_in.at[here], proj_sem, d, z * quad + spot)
+        )
+        proj_copies[-1].start()
+    proj_in[here] = proj_out[here]
+    for copy in proj_copies:
+        copy.wait()
+
+    square = jnp.zeros((block, 1), f32)
+    for q in range(slices):
+        value = x_ref[c, q].astype(f32)
+        for h in range(halves):
+            value = value + proj_in[(q // per) * halves + h, q % per]
+        hidden[q] = value
+        square = square + jnp.sum(value * value, axis=1, keepdims=True)
+    scale = lax.rsqrt(square / (slices * part) + 1e-05)
+    for q in range(slices):
+        norm_out[q] = (hidden[q] * scale * gain_ref[q]).astype(bf16)
+
+    norm_copies = []
+    for d in range(1, count):
+        peer = lax.rem(me + d, count)
+        norm_copies.append(send(norm_out.at[peer // quad], features.at[me], norm_sem, d, peer))
+        norm_copies[-1].start()
+    features[me] = norm_out[z]
+    for copy in route_copies:
+        copy.wait()
+    for copy in norm_copies:
+        copy.wait()
+    for load in loads:
+        load.wait()
+
+    def sums_copy(d):
+        target = lax.rem(z + d, slices)
+        return send(sums_out.at[target], sums_in.at[z], sums_sem, d, target * quad + here)
+
+    def marks(zone):
+        table = routing[pl.ds(zone * quad, quad)].reshape(quad * block, routing.shape[2])
+        return table
+
+    def up_step(i, carry):
+        d = lax.rem(i + 1, slices)
+        zone = lax.rem(z + d, slices)
+        value = features[pl.ds(zone * quad, quad)].reshape(quad * block, part)
+        table = marks(zone)
+        for g, matrix in enumerate((gate_ref, up_ref)):
+            picked = [jnp.zeros((quad * block, matrix.shape[2]), f32)] * top
+            for e in range(experts):
+                dense = jnp.dot(value, matrix[e], preferred_element_type=f32)
+                for k in range(top):
+                    picked[k] = jnp.where(table[:, k : k + 1] == float(e), dense, picked[k])
+            for k in range(top):
+                sums_out[zone, g * top + k] = picked[k].astype(bf16)
+
+        @pl.when(i < slices - 1)
+        def _():
+            sums_copy(d).start()
+
+        return carry
+
+    lax.fori_loop(0, slices, up_step, 0)
+    sums_in[z] = sums_out[z]
+    for d in range(1, slices):
+        sums_copy(d).wait()
+
+    table = marks(z)
+    for k in range(top):
+        gate = jnp.zeros(sums_in.shape[2:], f32)
+        up = jnp.zeros(sums_in.shape[2:], f32)
+        for q in range(slices):
+            gate = gate + sums_in[q, k].astype(f32)
+            up = up + sums_in[q, top + k].astype(f32)
+        value = gate / (1.0 + jnp.exp(-gate)) * up * table[:, top + k : top + k + 1]
+        act_all[z, k] = value.astype(bf16)
+
+    def act_copy(d):
+        target = lax.rem(z + d, slices)
+        return send(act_all.at[z], act_all.at[z], act_sem, d, target * quad + here)
+
+    for d in range(1, slices):
+        act_copy(d).start()
+
+    def down_copy(zone, d):
+        spot = lax.rem(here + d, quad)
+        return pltpu.make_async_remote_copy(
+            src_ref=down_out.at[zone, spot],
+            dst_ref=down_in.at[zone, here],
+            send_sem=down_sem.at[0, zone, d],
+            recv_sem=down_sem.at[1, zone, d],
+            device_id=device(z * quad + spot),
+            device_id_type=pl.DeviceIdType.MESH,
+        )
+
+    def down_step(i, carry):
+        zone = lax.rem(z - i + slices, slices)
+
+        @pl.when(i > 0)
+        def _():
+            act_copy(i).wait()
+
+        table = marks(zone)
+        total = jnp.zeros((quad * block, part), f32)
+        for e in range(experts):
+            spread = jnp.zeros(act_all.shape[2:], bf16)
+            for k in range(top):
+                spread = jnp.where(table[:, k : k + 1] == float(e), act_all[zone, k], spread)
+            total = total + lax.dot_general(
+                spread, down_ref[e], (((1,), (1,)), ((), ())), preferred_element_type=f32
+            )
+        down_out[zone] = total.reshape(quad, block, part)
+        for d in range(1, quad):
+            down_copy(zone, d).start()
+        return carry
+
+    lax.fori_loop(0, slices, down_step, 0)
+
+    def part_copy(d):
+        target = lax.rem(z + d, slices)
+        return send(part_out.at[target], part_in.at[z], part_sem, d, target * quad + here)
+
+    for i in range(slices):
+        zone = lax.rem(z - i + slices, slices)
+        down_in[zone, here] = down_out[zone, here]
+        for d in range(1, quad):
+            down_copy(zone, d).wait()
+        value = down_in[zone, 0]
+        for s in range(1, quad):
+            value = value + down_in[zone, s]
+        part_out[zone] = value
+        if i > 0:
+            part_copy((slices - i) % slices).start()
+    part_in[z] = part_out[z]
+    for d in range(1, slices):
+        part_copy(d).wait()
+    for q in range(slices):
+        final[q] = (hidden[q] + part_in[q]).astype(bf16)
+
+    share = slices // halves
+    swaps = []
+    for d in range(1, halves):
+        other = lax.rem(c + d, halves)
+        swaps.append(
+            send(
+                final.at[pl.ds(other * share, share)],
+                result_ref.at[c],
+                swap_sem,
+                d,
+                z * quad + x * halves + other,
+            )
+        )
+        swaps[-1].start()
+    result_ref[c] = final[pl.ds(c * share, share)]
+    for copy in swaps:
+        copy.wait()
+
+
+def move_tokens(
+    x_res,
+    query_new,
+    key_new,
+    value_new,
+    key_cache,
+    value_cache,
+    lengths,
+    routes,
+    route_weight,
+    norm_gain,
+    out_weight,
+    w_gate,
+    w_up,
+    w_down,
+):
+    slices = lax.axis_size("expert")
+    rows = lax.axis_size("dp")
+    halves = lax.axis_size("tensor")
+    experts, part, hidden_part = w_gate.shape
+    steps, tokens, width = x_res.shape
+    top = routes.shape[2]
+    mine = steps * tokens
+    block = mine // halves
+    quad = rows * halves
+    count = slices * quad
+    share = slices // halves
+    f32, bf16 = jnp.float32, jnp.bfloat16
+
+    packed = jnp.concatenate([routes.astype(f32), route_weight], axis=2)
+    packed = packed.reshape(halves, block, 2 * top)
+    packed = jnp.pad(packed, ((0, 0), (0, 0), (0, 128 - 2 * top)))
+    attended = attend_steps(query_new, key_cache, value_cache, key_new, value_new, lengths)
+    residual = x_res.reshape(halves, block, slices, part).transpose(0, 2, 1, 3)
+    gain = norm_gain.reshape(slices, 1, part)
+    per = out_weight.shape[1] // part
+    projection = out_weight.reshape(out_weight.shape[0], per, part).transpose(1, 0, 2)
+    vmem = pl.BlockSpec(memory_space=pltpu.VMEM)
+    anywhere = pl.BlockSpec(memory_space=pl.ANY)
+    dma = pltpu.SemaphoreType.DMA
+    result = pl.pallas_call(
+        functools.partial(layer_kernel, slices, rows, halves, top),
+        out_shape=jax.ShapeDtypeStruct((halves, share, block, part), bf16),
+        in_specs=[vmem] * 5 + [anywhere] * 3,
+        out_specs=vmem,
+        scratch_shapes=[
+            pltpu.VMEM(w_gate.shape, bf16),
+            pltpu.VMEM(w_up.shape, bf16),
+            pltpu.VMEM(w_down.shape, bf16),
+            pltpu.VMEM((count, block, 128), f32),
+            pltpu.VMEM((rows - 1,) + attended.shape, bf16),
+            pltpu.VMEM((quad, per, block, part), f32),
+            pltpu.VMEM((quad, per, block, part), f32),
+            pltpu.VMEM((slices, block, part), f32),
+            pltpu.VMEM((slices, block, part), bf16),
+            pltpu.VMEM((count, block, part), bf16),
+            pltpu.VMEM((slices, 2 * top, quad * block, hidden_part), bf16),
+            pltpu.VMEM((slices, 2 * top, quad * block, hidden_part), bf16),
+            pltpu.VMEM((slices, top, quad * block, hidden_part), bf16),
+            pltpu.VMEM((slices, quad, block, part), f32),
+            pltpu.VMEM((slices, quad, block, part), f32),
+            pltpu.VMEM((slices, block, part), f32),
+            pltpu.VMEM((slices, block, part), f32),
+            pltpu.VMEM((slices, block, part), bf16),
+            dma((3,)),
+            dma((2, rows)),
+            dma((2, count)),
+            dma((2, quad)),
+            dma((2, count)),
+            dma((2, slices)),
+            dma((2, slices)),
+            dma((2, slices, quad)),
+            dma((2, slices)),
+            dma((2, halves)),
+        ],
+        compiler_params=pltpu.CompilerParams(
+            collective_id=0, has_side_effects=True, vmem_limit_bytes=40 * 1024 * 1024
+        ),
+    )(attended, packed, residual, gain, projection, w_gate, w_up, w_down)
+    result = result.transpose(0, 2, 1, 3)
+    return result.reshape(steps, tokens, width // halves)
+
+
+def local(*args):
+    x_res, routes, w_gate = args[0], args[7], args[11]
+    spread = lax.axis_size("expert") * lax.axis_size("dp")
+    travelling = x_res.shape[0] * x_res.shape[1] * spread * routes.shape[2]
+    if travelling < w_gate.shape[0] * w_gate.shape[1]:
+        return move_tokens(*args)
+    return move_weights(*args)
+
+
 def solution(mesh):
     in_specs = (
         P(None, ("groups", "expert", "dp"), None),

time: 349 us -> 102 us (0.29)
  waiting for transfers between devices: 122 us -> 0 us
  blocking collectives: 117 us -> 0 us
  Pallas kernels: 0 us -> 85 us
  starting transfers between devices: 34.6 us -> 0 us
  matrix products: 25.6 us -> 1.2 us
  local copies, waits for them, and re-layouts: 28.6 us -> 12.4 us
  between operations: 13.9 us -> 0.12 us
    all_to_all x2 -> x0, blocking collectives: 110 us -> none  [the longest x1 57.2 us: local(): lax.all_to_all(doubled[2], 'expert', split_axis=0, concat_axis=2, tiled=T...]
    all_to_all x8 -> x0, waiting for transfers between devices: 103 us -> none  [the longest x1 34.2 us: local(): lax.all_to_all(doubled[0], 'expert', split_axis=0, concat_axis=2, tiled=T...]
    pallas_call x0 -> x1, Pallas kernels: none -> 85 us  [move_tokens(): pl.pallas_call(functools.partial(layer_kernel, slices, rows, halves, top)...]
    all_to_all x8 -> x0, starting transfers between devices: 34.5 us -> none  [the longest x2 9.69 us: local(): lax.all_to_all(outgoing.reshape(expert_count * row_count, slot_count, wid...]
    dot_general x18 -> x2, matrix products: 25.6 us -> 1.2 us  [the longest x1 0.96 us: attend_steps(): jnp.einsum('bgrc,bcgd->bgrd', probs, values, preferred_element_type=jnp.f...]
    psum x1 -> x0, waiting for transfers between devices: 18.3 us -> none  [local(): lax.psum(partial_value, 'tensor')]
    all_to_all x6 -> x0, local copies, waits for them, and re-layouts: 18.2 us -> none  [the longest x1 4.21 us: local(): lax.all_to_all(lax.all_to_all(doubled[1], 'expert', split_axis=0, concat_...]
    psum x1 -> x0, blocking collectives: 7.2 us -> none  [local(): expert_out = lax.psum(partial_out, 'tensor').astype(jnp.bfloat16)]
  transfers between devices with their start and end apart: 10 -> 0, of which waited for: 9 -> 0; matrix products, arithmetic and copies ran while one was open for 14% -> 0% of each run, Pallas kernels for 0% -> 0%
where the time goes in v2:
time: 102 us
  Pallas kernels  85 us (83%)
  local copies, waits for them, and re-layouts  12.4 us (12%)
  other arithmetic  2.83 us (3%)
  matrix products  1.2 us (1%)
    pallas_call x1, Pallas kernels, move_tokens(): pl.pallas_call(functools.partial(layer_kernel, slices, rows, halves, top)...  85 us
    unnamed x13, local copies, waits for them, and re-layouts  7.05 us

profile of v2, /device:TPU:0, one launch (start us, length us, event | category | flops | bytes accessed | tf_op | source)
XLA Modules:
  0.0 101.6 jit_solution(837402250080926824)
XLA Ops:
  0.0 0.0 copy-start.4
  0.0 0.8 iota_compare_fusion.1
  0.8 0.7 convert_element_type.13
  1.5 0.8 reshape.139.gain_ref
  2.3 0.7 copy.56
  3.0 0.7 copy.55
  3.7 0.1 copy.40
  3.8 0.8 copy.41
  4.5 0.1 select_maximum_fusion.packed_ref
  4.6 1.0 %reshape.138 = bf16[2,16,4,360]{3,2,1,0:T(4,128)(2,1)S(1)} reshape(bf16[2,16,1440]{2,1,0:T(8,128)(2,1)} %param.14) | data formatting | bytes 184320 | tf_op jit(solution)/shard_map/reshape | solution.py:510
  5.7 1.0 reshape.133
  6.7 1.0 pad_maximum_fusion.1
  7.7 0.3 copy.38
  8.0 0.0 copy-done.4
  8.0 0.0 copy-start.3
  8.1 0.3 copy.35
  8.4 0.2 fusion.3
  8.6 0.3 fusion.10
  8.9 1.0 fusion.5
  9.9 0.1 reshape.137.att_ref
  10.0 0.0 copy-done.3
  10.0 0.9 copy.43
  10.9 0.0 copy-start
  10.9 1.6 %copy-done = bf16[8,360,360]{2,1,0:T(8,128)(2,1)S(1)} copy-done((bf16[8,360,360]{2,1,0:T(8,128)(2,1)S(1)}, bf16[8,360,360]{2,1,0:T(8,128)(2,1)}, u32[]{:S(2)}) %copy-start) | copy-done | bytes 2073624
  12.5 0.0 copy-start.1
  12.5 1.6 %copy-done.1 = bf16[8,360,360]{2,1,0:T(8,128)(2,1)S(1)} copy-done((bf16[8,360,360]{2,1,0:T(8,128)(2,1)S(1)}, bf16[8,360,360]{2,1,0:T(8,128)(2,1)}, u32[]{:S(2)}) %copy-start.1) | copy-done | bytes 2073624
  14.1 0.0 copy-start.2
  14.1 1.6 %copy-done.2 = bf16[8,360,360]{2,1,0:T(8,128)(2,1)S(1)} copy-done((bf16[8,360,360]{2,1,0:T(8,128)(2,1)S(1)}, bf16[8,360,360]{2,1,0:T(8,128)(2,1)}, u32[]{:S(2)}) %copy-start.2) | copy-done | bytes 2073624
  15.8 85.0 %shard_map.136 = bf16[2,2,16,360]{3,2,1,0:T(8,128)(2,1)S(1)} custom-call(bf16[32,1024]{1,0:T(8,128)(2,1)S(1)} %reshape.137.att_ref, f32[2,16,128]{2,1,0:T(8,128)S(1)} %select_maximum_fusion.packed_ref, bf16[2,4,16,360]{3,2,1,0:T(8,128)(2,1)S(1)} %bitcast.37, f32[4,1,360]{2,1,0:T(1,128)S(1)} %reshape.139.gain_ref, bf16[2,1024,360]{2,1,0:T(8,128)(2,1)S(1)} %bitcast.36, ...), custom_call_target="tpu_custom_call" | custom-call | tf_op jit(solution)/shard_map/pallas_call | solution.py:517
  100.8 0.7 reshape.141
  (8 shorter events, 0.1 us)
Async XLA Ops:
  0.0 8.0 %copy-start.4 = (bf16[16,64,128]{2,1,0:T(8,128)(2,1)S(1)}, bf16[16,64,128]{2,1,0:T(8,128)(2,1)}, u32[]{:S(2)}) copy-start(bf16[16,64,128]{2,1,0:T(8,128)(2,1)} %param.18) | copy-start | bytes 786436
  8.0 2.0 %copy-start.3 = (bf16[1024,720]{0,1:T(8,128)(2,1)S(1)}, bf16[1024,720]{0,1:T(8,128)(2,1)}, u32[]{:S(2)}) copy-start(bf16[1024,720]{0,1:T(8,128)(2,1)} %param.24) | copy-start | bytes 4423684
  10.9 1.6 %copy-start = (bf16[8,360,360]{2,1,0:T(8,128)(2,1)S(1)}, bf16[8,360,360]{2,1,0:T(8,128)(2,1)}, u32[]{:S(2)}) copy-start(bf16[8,360,360]{2,1,0:T(8,128)(2,1)} %gate_hbm.1) | copy-start | bytes 6220804
  12.5 1.6 %copy-start.1 = (bf16[8,360,360]{2,1,0:T(8,128)(2,1)S(1)}, bf16[8,360,360]{2,1,0:T(8,128)(2,1)}, u32[]{:S(2)}) copy-start(bf16[8,360,360]{2,1,0:T(8,128)(2,1)} %up_hbm.1) | copy-start | bytes 6220804
  14.1 1.6 %copy-start.2 = (bf16[8,360,360]{2,1,0:T(8,128)(2,1)S(1)}, bf16[8,360,360]{2,1,0:T(8,128)(2,1)}, u32[]{:S(2)}) copy-start(bf16[8,360,360]{2,1,0:T(8,128)(2,1)} %down_hbm.1) | copy-start | bytes 6220804

commit v3 on v2

--- a/solution.py
+++ b/solution.py
@@ -230,6 +230,7 @@
     hidden,
     norm_out,
     features,
+    partial,
     sums_out,
     sums_in,
     act_all,
@@ -350,17 +351,55 @@
     for load in loads:
         load.wait()
 
-    def sums_copy(d):
-        target = lax.rem(z + d, slices)
-        return send(sums_out.at[target], sums_in.at[z], sums_sem, d, target * quad + here)
+    near = slices // 2
+
+    def neighbour(step):
+        return lax.rem(z + step + slices, slices) * quad + here
+
+    def sums_copy(zone, g):
+        span = pl.ds(g * top, top)
+        return pltpu.make_async_remote_copy(
+            src_ref=sums_out.at[zone, span],
+            dst_ref=sums_in.at[zone, span],
+            send_sem=sums_sem.at[0, zone, g],
+            recv_sem=sums_sem.at[1, zone, g],
+            device_id=device(neighbour(2 * (zone // near) - 1)),
+            device_id_type=pl.DeviceIdType.MESH,
+        )
+
+    def act_copy(zone):
+        return send(
+            act_all.at[zone], act_all.at[zone], act_sem, zone, neighbour(1 - 2 * (zone // near))
+        )
+
+    def owner(zone):
+        return (zone // near) * (slices - 1)
+
+    def source(zone):
+        return slices - 1 - owner(zone)
 
     def marks(zone):
-        table = routing[pl.ds(zone * quad, quad)].reshape(quad * block, routing.shape[2])
-        return table
+        return routing[pl.ds(zone * quad, quad)].reshape(quad * block, routing.shape[2])
+
+    def relay(zone):
+        @pl.when((z != owner(zone)) & (z != source(zone)))
+        def _():
+            for g in range(2):
+                sums_copy(zone, g).wait_recv()
+                for k in range(g * top, (g + 1) * top):
+                    sums_out[zone, k] = (partial[zone, k] + sums_in[zone, k].astype(f32)).astype(
+                        bf16
+                    )
+                sums_copy(zone, g).start()
+
+    def far_zone(i):
+        return lax.rem(i + (1 - z // near) * near, slices)
+
+    def near_zone(i):
+        return lax.rem(i + (z // near) * near, slices)
 
     def up_step(i, carry):
-        d = lax.rem(i + 1, slices)
-        zone = lax.rem(z + d, slices)
+        zone = far_zone(i)
         value = features[pl.ds(zone * quad, quad)].reshape(quad * block, part)
         table = marks(zone)
         for g, matrix in enumerate((gate_ref, up_ref)):
@@ -370,35 +409,22 @@
                 for k in range(top):
                     picked[k] = jnp.where(table[:, k : k + 1] == float(e), dense, picked[k])
             for k in range(top):
-                sums_out[zone, g * top + k] = picked[k].astype(bf16)
-
-        @pl.when(i < slices - 1)
+                partial[zone, g * top + k] = picked[k]
+
+            @pl.when(z == source(zone))
+            def _():
+                for k in range(g * top, (g + 1) * top):
+                    sums_out[zone, k] = partial[zone, k].astype(bf16)
+                sums_copy(zone, g).start()
+
+        @pl.when(i > 0)
         def _():
-            sums_copy(d).start()
+            relay(far_zone(i + slices - 1))
 
         return carry
 
     lax.fori_loop(0, slices, up_step, 0)
-    sums_in[z] = sums_out[z]
-    for d in range(1, slices):
-        sums_copy(d).wait()
-
-    table = marks(z)
-    for k in range(top):
-        gate = jnp.zeros(sums_in.shape[2:], f32)
-        up = jnp.zeros(sums_in.shape[2:], f32)
-        for q in range(slices):
-            gate = gate + sums_in[q, k].astype(f32)
-            up = up + sums_in[q, top + k].astype(f32)
-        value = gate / (1.0 + jnp.exp(-gate)) * up * table[:, top + k : top + k + 1]
-        act_all[z, k] = value.astype(bf16)
-
-    def act_copy(d):
-        target = lax.rem(z + d, slices)
-        return send(act_all.at[z], act_all.at[z], act_sem, d, target * quad + here)
-
-    for d in range(1, slices):
-        act_copy(d).start()
+    relay(far_zone(slices - 1))
 
     def down_copy(zone, d):
         spot = lax.rem(here + d, quad)
@@ -412,11 +438,26 @@
         )
 
     def down_step(i, carry):
-        zone = lax.rem(z - i + slices, slices)
-
-        @pl.when(i > 0)
+        zone = near_zone(i)
+
+        @pl.when(z == owner(zone))
         def _():
-            act_copy(i).wait()
+            table = marks(zone)
+            for g in range(2):
+                sums_copy(zone, g).wait_recv()
+            for k in range(top):
+                gate = partial[zone, k] + sums_in[zone, k].astype(f32)
+                up = partial[zone, top + k] + sums_in[zone, top + k].astype(f32)
+                value = gate / (1.0 + jnp.exp(-gate)) * up * table[:, top + k : top + k + 1]
+                act_all[zone, k] = value.astype(bf16)
+
+        @pl.when(z != owner(zone))
+        def _():
+            act_copy(zone).wait_recv()
+
+        @pl.when(z != source(zone))
+        def _():
+            act_copy(zone).start()
 
         table = marks(zone)
         total = jnp.zeros((quad * block, part), f32)
@@ -433,6 +474,20 @@
         return carry
 
     lax.fori_loop(0, slices, down_step, 0)
+
+    def settle(zone, carry):
+        @pl.when(z != owner(zone))
+        def _():
+            for g in range(2):
+                sums_copy(zone, g).wait_send()
+
+        @pl.when(z != source(zone))
+        def _():
+            act_copy(zone).wait_send()
+
+        return carry
+
+    lax.fori_loop(0, slices, settle, 0)
 
     def part_copy(d):
         target = lax.rem(z + d, slices)
@@ -530,6 +585,7 @@
             pltpu.VMEM((slices, block, part), f32),
             pltpu.VMEM((slices, block, part), bf16),
             pltpu.VMEM((count, block, part), bf16),
+            pltpu.VMEM((slices, 2 * top, quad * block, hidden_part), f32),
             pltpu.VMEM((slices, 2 * top, quad * block, hidden_part), bf16),
             pltpu.VMEM((slices, 2 * top, quad * block, hidden_part), bf16),
             pltpu.VMEM((slices, top, quad * block, hidden_part), bf16),
@@ -543,14 +599,14 @@
             dma((2, count)),
             dma((2, quad)),
             dma((2, count)),
-            dma((2, slices)),
+            dma((2, slices, 2)),
             dma((2, slices)),
             dma((2, slices, quad)),
             dma((2, slices)),
             dma((2, halves)),
         ],
         compiler_params=pltpu.CompilerParams(
-            collective_id=0, has_side_effects=True, vmem_limit_bytes=40 * 1024 * 1024
+            collective_id=0, has_side_effects=True, vmem_limit_bytes=60 * 1024 * 1024
         ),
     )(attended, packed, residual, gain, projection, w_gate, w_up, w_down)
     result = result.transpose(0, 2, 1, 3)
@@ -561,7 +617,8 @@
     x_res, routes, w_gate = args[0], args[7], args[11]
     spread = lax.axis_size("expert") * lax.axis_size("dp")
     travelling = x_res.shape[0] * x_res.shape[1] * spread * routes.shape[2]
-    if travelling < w_gate.shape[0] * w_gate.shape[1]:
+    even = lax.axis_size("expert") % 2 == 0
+    if even and travelling < w_gate.shape[0] * w_gate.shape[1]:
         return move_tokens(*args)
     return move_weights(*args)
 

time: 102 us -> 103 us (level)
  Pallas kernels: 85 us -> 87.3 us
  local copies, waits for them, and re-layouts: 12.4 us -> 10.8 us
    unnamed x13 -> x7, local copies, waits for them, and re-layouts: 7.05 us -> 2.18 us
    pallas_call x1, Pallas kernels: 85 us -> 87.3 us  [move_tokens(): pl.pallas_call(functools.partial(layer_kernel, slices, rows, halves, top)...]
where the time goes in v3:
time: 103 us
  Pallas kernels  87.3 us (85%)
  local copies, waits for them, and re-layouts  10.8 us (10%)
  other arithmetic  3.44 us (3%)
  matrix products  1.2 us (1%)
    pallas_call x1, Pallas kernels, move_tokens(): pl.pallas_call(functools.partial(layer_kernel, slices, rows, halves, top)...  87.3 us
    unnamed x7, local copies, waits for them, and re-layouts  2.18 us

profile of v3, /device:TPU:0, one launch (start us, length us, event | category | flops | bytes accessed | tf_op | source)
XLA Modules:
  0.0 102.8 jit_solution(6689235244526432030)
XLA Ops:
  0.0 0.0 copy-start.1
  0.0 0.8 iota_compare_fusion.1
  0.8 0.7 convert_element_type.13
  1.5 1.4 %reshape.139.gain_ref = f32[4,1,360]{2,1,0:T(1,128)} reshape(f32[1440]{0:T(1024)} %param.23) | data formatting | bytes 11520 | tf_op jit(solution)/shard_map/reshape | solution.py:566
  2.8 0.7 copy.56
  3.5 0.7 copy.55
  4.2 0.1 copy.40
  4.3 0.8 copy.41
  5.1 0.7 select_maximum_fusion.packed_ref
  5.8 1.0 %reshape.138 = bf16[2,16,4,360]{3,2,1,0:T(4,128)(2,1)S(1)} reshape(bf16[2,16,1440]{2,1,0:T(8,128)(2,1)} %param.14) | data formatting | bytes 184320 | tf_op jit(solution)/shard_map/reshape | solution.py:565
  6.9 0.6 copy.54
  7.5 1.0 reshape.133
  8.5 1.0 pad_maximum_fusion.1
  9.5 0.3 copy.38
  9.8 0.0 copy-done.1
  9.8 0.0 copy-start
  9.8 0.3 copy.35
  10.2 0.2 fusion.3
  10.4 0.3 fusion.10
  10.7 1.0 fusion.5
  11.6 0.8 reshape.137.att_ref
  12.4 0.0 copy-done
  12.4 1.6 %copy.43 = bf16[1024,2,360]{2,0,1:T(8,128)(2,1)} copy(bf16[1024,2,360]{0,2,1:T(8,128)(2,1)S(1)} %bitcast.38) | data formatting | bytes 2949120 | tf_op jit(solution)/shard_map/reshape | solution.py:568
  14.0 87.3 %shard_map.136 = bf16[2,2,16,360]{3,2,1,0:T(8,128)(2,1)} custom-call(bf16[32,1024]{1,0:T(8,128)(2,1)} %reshape.137.att_ref, f32[2,16,128]{2,1,0:T(8,128)} %select_maximum_fusion.packed_ref, bf16[2,4,16,360]{3,2,1,0:T(8,128)(2,1)} %bitcast.41, f32[4,1,360]{2,1,0:T(1,128)} %reshape.139.gain_ref, bf16[2,1024,360]{2,1,0:T(8,128)(2,1)} %bitcast.36, ...), custom_call_target="tpu_custom_call" | custom-call | tf_op jit(solution)/shard_map/pallas_call | solution.py:572
  101.3 0.8 copy.44
  102.1 0.7 reshape.141
  (6 shorter events, 0.1 us)
Async XLA Ops:
  0.0 9.8 %copy-start.1 = (bf16[16,64,128]{2,1,0:T(8,128)(2,1)S(1)}, bf16[16,64,128]{2,1,0:T(8,128)(2,1)}, u32[]{:S(2)}) copy-start(bf16[16,64,128]{2,1,0:T(8,128)(2,1)} %param.18) | copy-start | bytes 786436
  9.8 2.6 %copy-start = (bf16[1024,720]{0,1:T(8,128)(2,1)S(1)}, bf16[1024,720]{0,1:T(8,128)(2,1)}, u32[]{:S(2)}) copy-start(bf16[1024,720]{0,1:T(8,128)(2,1)} %param.24) | copy-start | bytes 4423684

commit v4 on v3

--- a/solution.py
+++ b/solution.py
@@ -393,7 +393,10 @@
                 sums_copy(zone, g).start()
 
     def far_zone(i):
-        return lax.rem(i + (1 - z // near) * near, slices)
+        end = slices - 1
+        middle = 1 - z // end - (end - z) // end
+        turn = middle * ((i % 2) * near + i // 2) + (1 - middle) * i
+        return lax.rem(turn + (1 - z // near) * near, slices)
 
     def near_zone(i):
         return lax.rem(i + (z // near) * near, slices)
@@ -419,7 +422,7 @@
 
         @pl.when(i > 0)
         def _():
-            relay(far_zone(i + slices - 1))
+            relay(far_zone(i - 1))
 
         return carry
 

time: 103 us -> 94.8 us (0.920)
  Pallas kernels: 87.3 us -> 78.8 us
    pallas_call x1, Pallas kernels: 87.3 us -> 78.8 us  [move_tokens(): pl.pallas_call(functools.partial(layer_kernel, slices, rows, halves, top)...]
where the time goes in v4:
time: 94.8 us; the launch traced here: 94.3 us
  Pallas kernels  78.8 us (83%)
  local copies, waits for them, and re-layouts  10.8 us (11%)
  other arithmetic  3.44 us (4%)
  matrix products  1.2 us (1%)
    pallas_call x1, Pallas kernels, move_tokens(): pl.pallas_call(functools.partial(layer_kernel, slices, rows, halves, top)...  78.8 us
    unnamed x7, local copies, waits for them, and re-layouts  2.18 us

profile of v4, /device:TPU:0, one launch (start us, length us, event | category | flops | bytes accessed | tf_op | source)
XLA Modules:
  0.0 94.3 jit_solution(916634759668357396)
XLA Ops:
  0.0 0.0 copy-start.1
  0.0 0.8 iota_compare_fusion.1
  0.8 0.7 convert_element_type.13
  1.5 1.4 %reshape.139.gain_ref = f32[4,1,360]{2,1,0:T(1,128)} reshape(f32[1440]{0:T(1024)} %param.23) | data formatting | bytes 11520 | tf_op jit(solution)/shard_map/reshape | solution.py:569
  2.8 0.7 copy.56
  3.5 0.7 copy.55
  4.2 0.1 copy.40
  4.3 0.8 copy.41
  5.1 0.7 select_maximum_fusion.packed_ref
  5.8 1.0 %reshape.138 = bf16[2,16,4,360]{3,2,1,0:T(4,128)(2,1)S(1)} reshape(bf16[2,16,1440]{2,1,0:T(8,128)(2,1)} %param.14) | data formatting | bytes 184320 | tf_op jit(solution)/shard_map/reshape | solution.py:568
  6.9 0.6 copy.54
  7.5 1.0 %reshape.133 = bf16[2,16,2,8,64]{4,3,2,1,0:T(8,128)(2,1)S(1)} reshape(bf16[2,16,1024]{2,1,0:T(8,128)(2,1)} %param.15) | data formatting | bytes 131072 | tf_op jit(solution)/shard_map/reshape | solution.py:184
  8.5 1.0 %pad_maximum_fusion.1 = bf16[16,66,128]{2,1,0:T(8,128)(2,1)S(1)} fusion(bf16[16,2,128]{2,1,0:T(2,128)(2,1)S(1)} %bitcast.44, bf16[16,64,128]{2,1,0:T(8,128)(2,1)} %param.19), kind=kLoop, calls=%fused_computation.9 | loop fusion | flops 540672 | bytes 540672 | tf_op jit(solution)/shard_map/concatenate | solution.py:189
  9.5 0.3 copy.38
  9.8 0.0 copy-done.1
  9.8 0.0 copy-start
  9.8 0.3 copy.35
  10.2 0.2 fusion.3
  10.4 0.3 fusion.10
  10.7 1.0 %fusion.5 = bf16[16,2,2,8,64]{4,3,2,1,0:T(8,128)(2,1)S(1)} fusion(bf16[16,66,2,64]{1,3,2,0:T(8,128)(2,1)S(1)} %bitcast.39, f32[16,2,16]{2,1,0:T(2,128)S(1)} %fusion.10, f32[16,2,16,66]{3,2,1,0:T(8,128)S(1)} %fusion.3), kind=kOutput, calls=%fused_computation.7 | convolution fusion | flops 4460097 | bytes 473088 | tf_op jit(solution)/shard_map/bgrc,bcgd->bgrd/dot_general | solution.py:202
  11.6 0.8 reshape.137.att_ref
  12.4 0.0 copy-done
  12.4 1.6 %copy.43 = bf16[1024,2,360]{2,0,1:T(8,128)(2,1)} copy(bf16[1024,2,360]{0,2,1:T(8,128)(2,1)S(1)} %bitcast.38) | data formatting | bytes 2949120 | tf_op jit(solution)/shard_map/reshape | solution.py:571
  14.0 78.8 %shard_map.136 = bf16[2,2,16,360]{3,2,1,0:T(8,128)(2,1)} custom-call(bf16[32,1024]{1,0:T(8,128)(2,1)} %reshape.137.att_ref, f32[2,16,128]{2,1,0:T(8,128)} %select_maximum_fusion.packed_ref, bf16[2,4,16,360]{3,2,1,0:T(8,128)(2,1)} %bitcast.41, f32[4,1,360]{2,1,0:T(1,128)} %reshape.139.gain_ref, bf16[2,1024,360]{2,1,0:T(8,128)(2,1)} %bitcast.36, ...), custom_call_target="tpu_custom_call" | custom-call | tf_op jit(solution)/shard_map/pallas_call | solution.py:575
  92.8 0.8 copy.44
  93.6 0.7 reshape.141
  (6 shorter events, 0.1 us)
Async XLA Ops:
  0.0 9.8 %copy-start.1 = (bf16[16,64,128]{2,1,0:T(8,128)(2,1)S(1)}, bf16[16,64,128]{2,1,0:T(8,128)(2,1)}, u32[]{:S(2)}) copy-start(bf16[16,64,128]{2,1,0:T(8,128)(2,1)} %param.18) | copy-start | bytes 786436
  9.8 2.6 %copy-start = (bf16[1024,720]{0,1:T(8,128)(2,1)S(1)}, bf16[1024,720]{0,1:T(8,128)(2,1)}, u32[]{:S(2)}) copy-start(bf16[1024,720]{0,1:T(8,128)(2,1)} %param.24) | copy-start | bytes 4423684
